TPU v7x, 32 devices: a whole 2x2x4 slice. The times are simulated.
32 devices in a mesh: fsdp: 16 (over z, y, core), rep: 2 (over x).
Axes of the slice: x: 2, y: 2, z: 4, core: 2. Of those that a mesh axis runs over, the one named last changes fastest.
Arguments:
- block_input: bfloat16 [64, 128, 768], P(('fsdp', 'rep')), may hold values from -6 to 6
- span_lengths: int32 [64], P(('fsdp', 'rep')), may hold values from 32 to 128, as said below
- mlm_positions: int32 [64, 32], P(('fsdp', 'rep')), may hold values from 0 to 127, as said below
- mlm_labels: int32 [64, 32], P(('fsdp', 'rep')), may hold values from 0 to 30521
- span_pairs: int32 [64], P(('fsdp', 'rep')), may hold values from 0 to 63, as said below
- layer_mats: float32 [7077888], P(('fsdp', 'rep'))
- vectors: float32 [9216], P(('fsdp', 'rep'))
- embedding: float32 [23440896], P(('fsdp', 'rep'))
- mom1_mats: float32 [7077888], P(('fsdp', 'rep')), may hold values from -6 to 6
- mom2_mats: float32 [7077888], P(('fsdp', 'rep')), may hold values from 0.01 to 10
- mom1_vecs: float32 [9216], P(('fsdp', 'rep')), may hold values from -6 to 6
- mom2_vecs: float32 [9216], P(('fsdp', 'rep')), may hold values from 0.01 to 10
- mom1_embed: float32 [23440896], P(('fsdp', 'rep')), may hold values from -6 to 6
- mom2_embed: float32 [23440896], P(('fsdp', 'rep')), may hold values from 0.01 to 10
Outputs:
- grad_input: float32 [64, 128, 768], P(('fsdp', 'rep'))
- grad_mats: float32 [7077888], P(('fsdp', 'rep'))
- grad_vecs: float32 [9216], P(('fsdp', 'rep'))
- grad_embed: float32 [23440896], P(('fsdp', 'rep'))
- step_mats: float32 [7077888], P(('fsdp', 'rep'))
- step_vecs: float32 [9216], P(('fsdp', 'rep'))
- step_embed: float32 [23440896], P(('fsdp', 'rep'))
Inputs may be any that keep to these rules, and one draw needn't show every extreme that they name: `span_lengths`: A sequence's real tokens come first, padding after; some sequence has exactly 128 and some exactly 32 real tokens. `mlm_positions`: every slot's position lies below its sequence's span length; positions may repeat within a sequence; slot j of sequence s is used when j < span_lengths[s] // 4. span_pairs[span_pairs[s]] = s and span_pairs[s] != s for every s.
All inputs are finite; a program needn't handle non-finite values.
Results may differ from a plain program's by a relative error of at most 0.012.
The roundings to bfloat16 on the way count: a program that leaves them out, or rounds other values in their place, can miss the bound.
Values may be sent and summed in bfloat16 or wider, within the bound.
No kernel may reach another device: no remote copies, remote signals or barrier semaphores. Data moves between devices by JAX's collectives and lax.ppermute only.
A program may use at most 512 MiB of HBM per device.

v0:
```python
import functools
import math

import jax
import jax.numpy as jnp
from jax import lax
from jax.experimental import pallas as pl
from jax.experimental.pallas import tpu as pltpu
from jax.sharding import Mesh, PartitionSpec as P

D = 768
FF = 3072
HEAD_DIM = 64
VOCAB = 30522
ADAM_STEP = 10


norm_eps = 1e-12
beta_one = 0.9
beta_two = 0.999
adam_eps = 1e-06
decay_rate = 0.01


def split_mats(flat):
    first = 3 * D * D
    second = first + D * D
    third = second + D * FF
    return (
        flat[:first].reshape(D, 3 * D),
        flat[first:second].reshape(D, D),
        flat[second:third].reshape(D, FF),
        flat[third:].reshape(FF, D),
    )


def split_vecs(flat):
    widths_list = [D, D, D, D, D, FF, D, D, D]
    pieces = []
    offset = 0
    for piece_width in widths_list:
        pieces.append(flat[offset : offset + piece_width].astype(jnp.float32))
        offset = offset + piece_width
    return pieces


def center_scale(resid):
    center = resid - jnp.mean(resid, axis=-1, keepdims=True)
    inverse = lax.rsqrt(jnp.mean(center * center, axis=-1, keepdims=True) + norm_eps)
    return (center * inverse, inverse)


def norm_back(d_normed, normed, inverse):
    return inverse * (
        d_normed
        - jnp.mean(d_normed, axis=-1, keepdims=True)
        - normed * jnp.mean(d_normed * normed, axis=-1, keepdims=True)
    )


def gelu_slope(value):
    return (
        0.5 * (1.0 + lax.erf(value * 0.7071067811865476))
        + value * jnp.exp(-0.5 * value * value) * 0.3989422804014327
    )


def contract_rows(left, right):
    return lax.dot_general(
        left, right, (((0,), (0,)), ((), ())), preferred_element_type=jnp.float32
    )


def contract_cols(left, right):
    return lax.dot_general(
        left, right, (((1,), (1,)), ((), ())), preferred_element_type=jnp.float32
    )


def adam_step(weight, grad, first, second, step_float, decay):
    first_new = beta_one * first + (1.0 - beta_one) * grad
    second_new = beta_two * second + (1.0 - beta_two) * grad * grad
    first_hat = first_new / (1.0 - beta_one**step_float)
    second_hat = second_new / (1.0 - beta_two**step_float)
    return first_hat / (jnp.sqrt(second_hat) + adam_eps) + decay * weight


def flip(value, name):
    return lax.ppermute(value, name, [(0, 1), (1, 0)])


def gather_bits(shard, order, names):
    grown = shard
    for name in order:
        other = flip(grown, name)
        first = lax.axis_index(name) == 0
        grown = jnp.stack([jnp.where(first, grown, other), jnp.where(first, other, grown)])
    axes = list(reversed(order))
    rank = len(axes)
    turn = [axes.index(name) for name in names] + list(range(rank, grown.ndim))
    return grown.transpose(turn).reshape((2**rank,) + shard.shape)


def reduce_bits(blocks, order, names):
    left = list(names)
    held = blocks.reshape((2,) * len(left) + blocks.shape[1:])
    for name in order:
        axis = left.index(name)
        here = lax.axis_index(name)
        send = lax.dynamic_index_in_dim(held, 1 - here, axis, keepdims=False)
        keep = lax.dynamic_index_in_dim(held, here, axis, keepdims=False)
        other = flip(send, name)
        held = (keep.astype(jnp.float32) + other.astype(jnp.float32)).astype(blocks.dtype)
        left.remove(name)
    return held


def bit_orders(names, core):
    outer = [name for name in names if name != core]
    count = len(outer)
    if count == 4:
        picks = ((0, 3, 2, 1), (0, 2, 1, 3), (0, 1, 3, 2))
        return [[outer[k] for k in pick] + [core] for pick in picks]
    step = max(1, count // 3)
    return [outer[step * k :] + outer[: step * k] + [core] for k in range(3)]


def device_mask(name, names):
    return 1 << (len(names) - 1 - names.index(name))


def gather_relative(shards, orders, names, early=(), exchange=None, work=None):
    held = []
    for number, (shard, order) in enumerate(zip(shards, orders)):
        grown, masks = shard, [0]
        for k, name in enumerate(order[:-2]):
            grown = lax.optimization_barrier(jnp.concatenate([grown, flip(grown, name)]))
            if exchange is not None and k == 0 and number == len(orders) - 1:
                grown, given = lax.optimization_barrier((grown, early[-1]))
                early = (*early[:-1], exchange(given))
            masks = masks + [mask | device_mask(name, names) for mask in masks]
        held.append((grown, masks))
    grown_all = [grown for grown, _ in held]
    others = [flip(grown, order[-2]) for grown, order in zip(grown_all, orders)]
    if work is not None:
        late, early = lax.optimization_barrier((grown_all, early))
        grown_all, early = lax.optimization_barrier((late, work(*early)))
    gathered = []
    for grown, other, (_, masks), order in zip(grown_all, others, held, orders):
        bit = device_mask(order[-2], names)
        pieces = [(grown, masks), (other, [mask | bit for mask in masks])]
        bit = device_mask(order[-1], names)
        pieces = pieces + [
            (flip(piece, order[-1]), [mask | bit for mask in own]) for piece, own in pieces
        ]
        gathered.append(pieces)
    return gathered, early


def add_terms(terms):
    total = terms[0].astype(jnp.float32)
    for term in terms[1:]:
        total = total + term.astype(jnp.float32)
    return total


def reduce_relative(keeps, sends, orders, state=None, works=(), early_sums=None):
    works = dict(works)
    sends = list(sends)
    terms_all = [[keep] for keep in keeps]
    whole_all = [[keep] for keep in keeps]
    for step in range(len(orders[0])):
        for k, order in enumerate(orders):
            half = terms_all[k][0].shape[0] // 2
            if step == 0:
                urgent, rest = (flip(send, order[step]) for send in sends[k])
                whole_all[k].append(rest)
            else:
                other = flip(sends[k], order[step])
                urgent, rest = other[half:], other[:half]
                whole_all[k].append(other)
            if half:
                upper = [term[half:] for term in terms_all[k]] + [urgent]
                sends[k] = add_terms(upper).astype(urgent.dtype)
                terms_all[k] = [term[:half] for term in terms_all[k]] + [rest]
            else:
                terms_all[k] = terms_all[k] + [urgent]
        if step == early_sums:
            left = terms_all[0][0].shape[0]
            for k in range(len(orders)):
                sends[k], terms = lax.optimization_barrier((sends[k], whole_all[k]))
                terms_all[k] = [add_terms([term[:left] for term in terms])]
                whole_all[k] = list(terms_all[k])
        if step in works:
            sends[-1], state = lax.optimization_barrier((sends[-1], state))
            state = works[step](state)
    return whole_all, state


def dot_nn(left, right):
    return lax.dot_general(
        left, right, (((1,), (0,)), ((), ())), preferred_element_type=jnp.float32
    )


def interleave(count, rows):
    span = rows // count
    to = lax.broadcasted_iota(jnp.int32, (rows, rows), 0)
    source = lax.broadcasted_iota(jnp.int32, (rows, rows), 1)
    return (source == count * lax.rem(to, span) + lax.div(to, span)).astype(jnp.bfloat16)


def deinterleave(count, rows):
    span = rows // count
    source = lax.broadcasted_iota(jnp.int32, (rows, rows), 1)
    to = lax.broadcasted_iota(jnp.int32, (rows, rows), 0)
    return (to == count * lax.rem(source, span) + lax.div(source, span)).astype(jnp.bfloat16)


def valid_rows(len_ref, rows, seq_here):
    length = rows // seq_here
    row = lax.broadcasted_iota(jnp.int32, (rows, 1), 0)
    valid = jnp.zeros((rows, 1), jnp.float32)
    for seq in range(seq_here):
        inside = (row >= seq * length) & (row < seq * length + len_ref[seq])
        valid = jnp.where(inside, 1.0, valid)
    return valid


def stack_pair(value):
    lane = lax.broadcasted_iota(jnp.int32, value.shape, 1)
    zero = jnp.zeros_like(value)
    left = lane < HEAD_DIM
    return jnp.concatenate([jnp.where(left, value, zero), jnp.where(left, zero, value)], axis=0)


def join_pair(stacked):
    half = stacked.shape[0] // 2
    lane = lax.broadcasted_iota(jnp.int32, (half, stacked.shape[1]), 1)
    return jnp.where(lane < HEAD_DIM, stacked[:half], stacked[half:])


def pair_scores(stacked, keys, limit):
    raw = contract_cols(stacked, keys) * HEAD_DIM ** (-0.5)
    column = lax.broadcasted_iota(jnp.int32, raw.shape, 1)
    return jnp.where(column < limit, raw, -1e30)


def center_rows(resid):
    center = resid - jnp.mean(resid, axis=-1, keepdims=True)
    inverse = lax.rsqrt(jnp.mean(center * center, axis=-1, keepdims=True) + norm_eps)
    return center * inverse, inverse


def gelu_phi(value):
    return 0.5 * (1.0 + lax.erf(value * 0.7071067811865476))


def forward_kernel(plan, planes, seq_here, *refs):
    me_ref, len_ref, place_ref, x_ref, vec_ref = refs[:5]
    blocks = refs[5 : 5 + len(plan)]
    heads_refs = refs[5 + len(plan) : 8 + len(plan)]
    wall_ref, qkv_ref, att_ref, n1_ref, pre_ref, n2_ref, stat_ref = refs[
        8 + len(plan) : 15 + len(plan)
    ]
    raw, turned, qkv, att, n1, pre_all, in_sem, out_sem = refs[15 + len(plan) :]
    rows, width = x_ref.shape
    length = rows // seq_here
    pairs = width // (2 * HEAD_DIM)
    up = 4 * width
    me = me_ref[0]
    for first in (True, False):
        for (part, unit, masks), block in zip(plan, blocks):
            for place, mask in enumerate(masks):
                device = me ^ mask
                early = device < planes

                @pl.when(early if first else jnp.logical_not(early))
                def _(device=device, part=part, unit=unit, block=block, place=place, first=first):
                    row = pl.multiple_of((3 * device + part) * unit, 16)
                    pltpu.make_async_copy(
                        block.at[place], raw.at[pl.ds(row, unit)], in_sem.at[0 if first else 1]
                    ).start()

    copies = []

    def save(source, target):
        copy = pltpu.make_async_copy(source, target, out_sem.at[len(copies)])
        copy.start()
        copies.append(copy)

    valid = valid_rows(len_ref, rows, seq_here)
    x = (x_ref[...].astype(jnp.float32) * valid).astype(jnp.bfloat16)
    split3, split4 = interleave(3, 384), interleave(4, 256)
    arrived = raw.at[0 : 3 * width]
    pltpu.make_async_copy(arrived, arrived, in_sem.at[0]).wait()

    for b in range(width // 128):
        block = dot_nn(split3, raw[384 * b : 384 * b + 384, :]).astype(jnp.bfloat16)
        for p in range(3):
            turned[width * p + 128 * b : width * p + 128 * b + 128, :] = block[
                128 * p : 128 * p + 128
            ]
    save(turned.at[0 : 3 * width], wall_ref.at[0 : 3 * width])
    for p, bias in ((0, 0), (1, None), (2, 1)):
        value = dot_nn(x, turned[width * p : width * (p + 1), :])
        if bias is not None:
            value = value + vec_ref[bias : bias + 1, :]
        qkv[:, width * p : width * (p + 1)] = value.astype(jnp.bfloat16)
    save(qkv, qkv_ref)

    stats = jnp.zeros((2 * length, 128), jnp.float32)
    lane = lax.broadcasted_iota(jnp.int32, stats.shape, 1)
    for seq in range(seq_here):
        here = slice(seq * length, (seq + 1) * length)
        for g in range(pairs):
            cols = [slice(width * p + 128 * g, width * p + 128 * g + 128) for p in range(3)]
            query, key, value = (qkv[here, c] for c in cols)
            scores = pair_scores(stack_pair(query), key, len_ref[seq])
            top = jnp.max(scores, axis=-1, keepdims=True)
            expo = jnp.exp(scores - top)
            total = jnp.sum(expo, axis=-1, keepdims=True)
            stats = jnp.where(lane == seq * pairs + g, top + jnp.log(total), stats)
            probs = (expo / total).astype(jnp.bfloat16)
            att[here, 128 * g : 128 * g + 128] = join_pair(dot_nn(probs, value)).astype(
                jnp.bfloat16
            )
    save(att, att_ref)
    arrived = raw.at[3 * width : 3 * up]
    pltpu.make_async_copy(arrived, arrived, in_sem.at[1]).wait()
    save(raw.at[3 * width : up], wall_ref.at[3 * width : up])
    save(raw.at[2 * up : 3 * up], wall_ref.at[2 * up : 3 * up])

    branch = dot_nn(att[...], raw[3 * width : up, :]) + vec_ref[2:3, :]
    for b in range(width // 64):
        block = dot_nn(split4, raw[up + 256 * b : up + 256 * b + 256, :]).astype(jnp.bfloat16)
        for p in range(4):
            row = width * (3 + p) + 64 * b
            turned[row : row + 64, :] = block[64 * p : 64 * p + 64]
    save(turned.at[3 * width : 7 * width], wall_ref.at[up : 2 * up])
    normed, inverse = center_rows(x.astype(jnp.float32) + branch)
    n1[...] = normed
    save(n1, n1_ref)
    stat_one = seq_here * pairs
    hidden = normed * vec_ref[3:4, :] + vec_ref[4:5, :]
    hidden_low = hidden.astype(jnp.bfloat16)
    total = hidden + vec_ref[9:10, :]
    for p in range(4):
        pre = dot_nn(hidden_low, turned[width * (3 + p) : width * (4 + p), :])
        pre = pre + vec_ref[5 + p : 6 + p, :]
        pre_all[p] = pre
        save(pre_all.at[p], pre_ref.at[p])
        act = (pre * gelu_phi(pre)).astype(jnp.bfloat16)
        total = total + dot_nn(act, raw[2 * up + width * p : 2 * up + width * (p + 1), :])
    normed, inverse_two = center_rows(total)
    n2_ref[...] = normed
    wide = lax.broadcasted_iota(jnp.int32, (rows, 128), 1)
    ends = jnp.where(
        wide == stat_one, inverse, jnp.where(wide == stat_one + 1, inverse_two, 0.0)
    )
    stat_ref[0] = stats
    stat_ref[1] = ends
    output = ((normed * vec_ref[10:11, :] + vec_ref[11:12, :]) * valid).astype(jnp.bfloat16)
    spot = lax.broadcasted_iota(jnp.int32, (rows, place_ref.shape[1]), 0)
    choose = (spot == place_ref[...]).astype(jnp.bfloat16)
    heads = contract_rows(choose, output).astype(jnp.bfloat16)
    cut = width // 3
    for k, heads_ref in enumerate(heads_refs):
        heads_ref[0] = heads[:, k * cut : (k + 1) * cut]
    for copy in copies:
        copy.wait()


def send_block(source, sinks, spots, device, part, out_sem):
    spot = spots[3 * device + part]
    half = sinks[0].shape[0]

    def copy(sink, place):
        pltpu.make_async_copy(source, sink.at[place], out_sem).start()

    keep, urgent, rest = sinks[3 * part : 3 * part + 3]
    pl.when(spot < half)(functools.partial(copy, keep, spot))
    pl.when((spot >= half) & (spot < half + half // 2))(
        functools.partial(copy, rest, spot - half)
    )
    pl.when(spot >= half + half // 2)(functools.partial(copy, urgent, spot - half - half // 2))


def sink_shapes(devices, block, dtype):
    half = devices // 2
    return [
        jax.ShapeDtypeStruct((count,) + block, dtype)
        for _ in range(3)
        for count in (half, half // 2, half // 2)
    ]


def wait_sinks(sinks, out_sem):
    for sink in sinks:
        pltpu.make_async_copy(sink, sink, out_sem).wait()


def backward_kernel(unit, seq_here, *refs):
    len_ref, spots, place_ref, x_ref, vec_ref, top_ref = refs[:6]
    wall_ref, qkv_ref, att_ref, n1_ref, pre_ref, n2_ref, stat_ref = refs[6:13]
    gin_ref, dvec_ref = refs[13:15]
    sinks = refs[15:24]
    wall, grads, parts, dqkv, qkv, att, n1, pre_all, in_sem, out_sem = refs[24:]
    rows, width = x_ref.shape
    length = rows // seq_here
    pairs = width // (2 * HEAD_DIM)
    low = jnp.bfloat16
    up = 4 * width
    ranges = [(n1_ref, n1)]
    for p in range(4):
        for first in (2 * up, up):
            rows_p = slice(first + width * p, first + width * (p + 1))
            ranges.append((wall_ref.at[rows_p], wall.at[rows_p]))
        ranges.append((pre_ref.at[p], pre_all.at[p]))
    out = slice(3 * width, up)
    ranges += [(att_ref, att), (wall_ref.at[out], wall.at[out]), (qkv_ref, qkv)]
    ranges += [(wall_ref.at[0 : 3 * width], wall.at[0 : 3 * width])]
    loads = [
        pltpu.make_async_copy(source, target, in_sem.at[k])
        for k, (source, target) in enumerate(ranges)
    ]
    for load in loads:
        load.start()

    def emit(first, last):
        for u in range(first // unit, last // unit):
            block = grads.at[u * unit : (u + 1) * unit]
            send_block(block, sinks, spots, u // 3, u % 3, out_sem)

    valid = valid_rows(len_ref, rows, seq_here)
    x = (x_ref[...].astype(jnp.float32) * valid).astype(low)
    stat_one = seq_here * pairs
    wide = lax.broadcasted_iota(jnp.int32, (rows, 128), 1)
    ends = stat_ref[1]
    inverse_one = jnp.sum(jnp.where(wide == stat_one, ends, 0.0), axis=-1, keepdims=True)
    inverse_two = jnp.sum(jnp.where(wide == stat_one + 1, ends, 0.0), axis=-1, keepdims=True)

    spot = lax.broadcasted_iota(jnp.int32, (rows, place_ref.shape[1]), 0)
    choose = (spot == place_ref[...]).astype(jnp.float32)
    d_output = valid * lax.dot_general(
        choose,
        top_ref[...],
        (((1,), (0,)), ((), ())),
        precision=lax.Precision.HIGHEST,
        preferred_element_type=jnp.float32,
    )
    normed = n2_ref[...]

    def sums(row, value):
        dvec_ref[row : row + 1, :] = jnp.sum(value, axis=0, keepdims=True)

    sums(10, d_output * normed)
    sums(11, d_output)
    d_resid = norm_back(d_output * vec_ref[10:11, :], normed, inverse_two)
    d_ffn = d_resid.astype(low)
    sums(9, d_ffn.astype(jnp.float32))
    d_hidden = d_resid
    loads[0].wait()
    normed = n1[...]
    hidden_low = (normed * vec_ref[3:4, :] + vec_ref[4:5, :]).astype(low)
    for p in range(4):
        for load in loads[1 + 3 * p : 4 + 3 * p]:
            load.wait()
        pre = pre_all[p]
        phi = gelu_phi(pre)
        act = (pre * phi).astype(low)
        down = slice(2 * up + width * p, 2 * up + width * (p + 1))
        grads[down, :] = contract_rows(act, d_ffn).astype(low)
        emit(down.start, down.stop)
        slope = phi + pre * jnp.exp(-0.5 * pre * pre) * 0.3989422804014327
        d_pre = (contract_cols(d_ffn, wall[down, :]) * slope).astype(low)
        sums(5 + p, d_pre.astype(jnp.float32))
        parts[width * p : width * (p + 1), :] = contract_rows(hidden_low, d_pre).astype(low)
        d_hidden = d_hidden + contract_cols(d_pre, wall[up + width * p : up + width * (p + 1), :])
    merge4 = deinterleave(4, 256)
    for b in range(width // 64):
        block = jnp.concatenate(
            [parts[width * p + 64 * b : width * p + 64 * b + 64, :] for p in range(4)], axis=0
        )
        grads[up + 256 * b : up + 256 * b + 256, :] = dot_nn(merge4, block).astype(low)
        if b % 3 == 2:
            emit(up + 256 * (b - 2), up + 256 * (b + 1))

    sums(3, d_hidden * normed)
    sums(4, d_hidden)
    d_resid = norm_back(d_hidden * vec_ref[3:4, :], normed, inverse_one)
    d_branch = d_resid.astype(low)
    sums(2, d_branch.astype(jnp.float32))
    for load in loads[13:]:
        load.wait()
    grads[3 * width : up, :] = contract_rows(att[...], d_branch).astype(low)
    emit(3 * width, up)
    d_att = contract_cols(d_branch, wall[3 * width : up, :]).astype(low)
    lane = lax.broadcasted_iota(jnp.int32, (2 * length, 128), 1)
    stats = stat_ref[0]
    for seq in range(seq_here):
        here = slice(seq * length, (seq + 1) * length)
        for g in range(pairs):
            cols = [slice(width * p + 128 * g, width * p + 128 * g + 128) for p in range(3)]
            query, key, value = (qkv[here, c] for c in cols)
            query = stack_pair(query)
            log_sum = jnp.sum(
                jnp.where(lane == seq * pairs + g, stats, 0.0), axis=-1, keepdims=True
            )
            probs = jnp.exp(pair_scores(query, key, len_ref[seq]) - log_sum)
            d_heads = stack_pair(d_att[here, 128 * g : 128 * g + 128])
            d_probs = contract_cols(d_heads, value)
            dqkv[here, cols[2]] = contract_rows(probs.astype(low), d_heads).astype(low)
            delta = jnp.sum(d_probs * probs, axis=-1, keepdims=True)
            d_scores = (probs * (d_probs - delta)).astype(low)
            scale = HEAD_DIM ** (-0.5)
            dqkv[here, cols[0]] = (join_pair(dot_nn(d_scores, key)) * scale).astype(low)
            dqkv[here, cols[1]] = (contract_rows(d_scores, query) * scale).astype(low)
    sums(0, dqkv[:, :width].astype(jnp.float32))
    sums(1, dqkv[:, 2 * width :].astype(jnp.float32))
    for p in range(3):
        d_part = dqkv[:, width * p : width * (p + 1)]
        parts[width * p : width * (p + 1), :] = contract_rows(x, d_part).astype(low)
    merge3 = deinterleave(3, 384)
    for b in range(width // 128):
        block = jnp.concatenate(
            [parts[width * p + 128 * b : width * p + 128 * b + 128, :] for p in range(3)], axis=0
        )
        grads[384 * b : 384 * b + 384, :] = dot_nn(merge3, block).astype(low)
        if b % 2 == 1:
            emit(384 * (b - 1), 384 * (b + 1))
    total = d_resid
    for p in range(3):
        d_part = dqkv[:, width * p : width * (p + 1)]
        total = total + contract_cols(d_part, wall[width * p : width * (p + 1), :])
    gin_ref[...] = total * valid
    wait_sinks(sinks, out_sem)


def call_forward(me, lengths, places, rows, vecs, gathered, devices, seq_here):
    count, width = rows.shape
    pieces = [(part, piece, masks) for part, own in enumerate(gathered) for piece, masks in own]
    plan = tuple((part, piece.shape[1], tuple(masks)) for part, piece, masks in pieces)
    total = 12 * width
    vmem = pl.BlockSpec(memory_space=pltpu.VMEM)
    smem = pl.BlockSpec(memory_space=pltpu.SMEM)
    hbm = pl.BlockSpec(memory_space=pl.ANY)
    low, full = jnp.bfloat16, jnp.float32
    outs = pl.pallas_call(
        functools.partial(forward_kernel, plan, devices // 4, seq_here),
        out_shape=[
            *[jax.ShapeDtypeStruct((1, places.shape[1], width // 3), low)] * 3,
            jax.ShapeDtypeStruct((total, width), low),
            jax.ShapeDtypeStruct((count, 3 * width), low),
            jax.ShapeDtypeStruct((count, width), low),
            jax.ShapeDtypeStruct((count, width), full),
            jax.ShapeDtypeStruct((4, count, width), full),
            jax.ShapeDtypeStruct((count, width), full),
            jax.ShapeDtypeStruct((2, count, 128), full),
        ],
        in_specs=[smem, smem, vmem, vmem, vmem] + [hbm] * len(pieces),
        out_specs=[vmem] * 3 + [hbm] * 5 + [vmem] * 2,
        scratch_shapes=[
            pltpu.VMEM((total, width), low),
            pltpu.VMEM((7 * width, width), low),
            pltpu.VMEM((count, 3 * width), low),
            pltpu.VMEM((count, width), low),
            pltpu.VMEM((count, width), full),
            pltpu.VMEM((4, count, width), full),
            pltpu.SemaphoreType.DMA((2,)),
            pltpu.SemaphoreType.DMA((11,)),
        ],
        compiler_params=pltpu.CompilerParams(vmem_limit_bytes=58 * 2**20),
        cost_estimate=pl.CostEstimate(
            flops=2 * count * total * width, bytes_accessed=48 * 2**20, transcendentals=0
        ),
    )(me, lengths, places, rows, vecs, *[piece for _, piece, _ in pieces])
    return *outs[:3], outs[3:]


def call_backward(lengths, spots, places, rows, vecs, top, saved, unit, seq_here):
    count, width = rows.shape
    total = 12 * width
    vmem = pl.BlockSpec(memory_space=pltpu.VMEM)
    smem = pl.BlockSpec(memory_space=pltpu.SMEM)
    hbm = pl.BlockSpec(memory_space=pl.ANY)
    low, full = jnp.bfloat16, jnp.float32
    return pl.pallas_call(
        functools.partial(backward_kernel, unit, seq_here),
        out_shape=[
            jax.ShapeDtypeStruct((count, width), full),
            jax.ShapeDtypeStruct((12, width), full),
        ]
        + sink_shapes(total // unit // 3, (unit, width), low),
        in_specs=[smem, smem, vmem, vmem, vmem, vmem] + [hbm] * 5 + [vmem] * 2,
        out_specs=[vmem, vmem] + [hbm] * 9,
        scratch_shapes=[
            pltpu.VMEM((total, width), low),
            pltpu.VMEM((total, width), low),
            pltpu.VMEM((4 * width, width), low),
            pltpu.VMEM((count, 3 * width), low),
            pltpu.VMEM((count, 3 * width), low),
            pltpu.VMEM((count, width), low),
            pltpu.VMEM((count, width), full),
            pltpu.VMEM((4, count, width), full),
            pltpu.SemaphoreType.DMA((17,)),
            pltpu.SemaphoreType.DMA,
        ],
        compiler_params=pltpu.CompilerParams(vmem_limit_bytes=58 * 2**20),
        cost_estimate=pl.CostEstimate(
            flops=4 * count * total * width, bytes_accessed=48 * 2**20, transcendentals=0
        ),
    )(lengths, spots, places, rows, vecs, top, *saved)


def turn_lanes(shift, width):
    source = lax.broadcasted_iota(jnp.int32, (width, width), 0) + shift
    source = jnp.where(source >= width, source - width, source)
    return (source == lax.broadcasted_iota(jnp.int32, (width, width), 1)).astype(jnp.bfloat16)


def table_kernel(embed_here, shift_ref, rows_ref, ends_ref, table_ref, owned_ref, tall):
    count, width = table_ref.shape
    here = rows_ref.shape[0]
    shift = shift_ref[0]
    tall[here:, :] = jnp.zeros((tall.shape[0] - here, width), jnp.float32)
    tall[8 : 8 + here, :] = rows_ref[...].astype(jnp.float32)
    tall[7:8, :] = ends_ref[0:1, :]
    tall[7 + here : 8 + here, :] = tall[7 + here : 8 + here, :] + ends_ref[1:2, :]
    tall[8 + here : 9 + here, :] = ends_ref[2:3, :]
    lane = lax.broadcasted_iota(jnp.int32, (count, width), 1)
    rolled = jnp.where(lane < width - shift, tall[8 : 8 + count, :], tall[7 : 7 + count, :])
    table = dot_nn(rolled.astype(jnp.bfloat16), turn_lanes(shift, width))
    start = lax.broadcasted_iota(jnp.int32, (count, 1), 0) * width - shift
    owned = (start >= 0) & (start < embed_here)
    table_ref[...] = table.astype(jnp.bfloat16)
    owned_ref[...] = jnp.where(owned, table, 0.0).astype(jnp.bfloat16)


def call_table(shift, rows, ends, count, embed_here):
    width = rows.shape[1]
    vmem = pl.BlockSpec(memory_space=pltpu.VMEM)
    smem = pl.BlockSpec(memory_space=pltpu.SMEM)
    return pl.pallas_call(
        functools.partial(table_kernel, embed_here),
        out_shape=[jax.ShapeDtypeStruct((count, width), jnp.bfloat16)] * 2,
        in_specs=[smem, vmem, vmem],
        out_specs=[vmem] * 2,
        scratch_shapes=[pltpu.VMEM((count + 16, width), jnp.float32)],
        compiler_params=pltpu.CompilerParams(vmem_limit_bytes=22 * 2**20),
        cost_estimate=pl.CostEstimate(
            flops=32 * count * width * width, bytes_accessed=40 * 2**20, transcendentals=0
        ),
    )(shift, rows, ends)


def eye_mask():
    return lax.broadcasted_iota(jnp.int32, (128, 128), 0) == lax.broadcasted_iota(
        jnp.int32, (128, 128), 1
    )


def to_row(column, eye):
    return jnp.concatenate(
        [
            jnp.sum(jnp.where(eye, column[k : k + 128], 0.0), axis=0, keepdims=True)
            for k in range(0, column.shape[0], 128)
        ],
        axis=1,
    )


def to_column(row, eye):
    return jnp.concatenate(
        [
            jnp.sum(jnp.where(eye, row[:, k : k + 128], 0.0), axis=1, keepdims=True)
            for k in range(0, row.shape[1], 128)
        ],
        axis=0,
    )


def logits_kernel(plan, embed_here, picks, span, *refs):
    me_ref, shift_ref, table_ref = refs[:3]
    blocks = refs[3 : 3 + len(plan)]
    picked_ref, expo_ref, stat_ref, top_ref, picked, expo_all, in_sem, out_sem = refs[
        3 + len(plan) :
    ]
    count, width = table_ref.shape
    me, shift = me_ref[0], shift_ref[0]
    group = 4
    for (part, masks), block in zip(plan, blocks):
        cols = pl.ds(part * block.shape[2], block.shape[2])
        for place, mask in enumerate(masks):
            device = me ^ mask
            pltpu.make_async_copy(
                block.at[place], picked.at[device, :, cols], in_sem
            ).start()
    whole = embed_here // width // 128 * 128
    eye = eye_mask()
    row_start = lax.broadcasted_iota(jnp.int32, (1, count), 1) * width - shift
    touched = (row_start < embed_here)[:, whole:]
    owned = (row_start >= 0)[:, :128]
    tops, sums, copies = [], [], []

    def save(source, target):
        copies.append(pltpu.make_async_copy(source, target, out_sem.at[len(copies)]))
        copies[-1].start()

    step = group * picks
    pltpu.make_async_copy(picked, picked, in_sem).wait()
    save(picked, picked_ref)
    for k in range(picked.shape[0] // group):
        here = slice(k * step, (k + 1) * step)
        rows = jnp.concatenate([picked[group * k + d, :picks, :] for d in range(group)], axis=0)
        logits = contract_cols(rows, table_ref[...])
        logits = jnp.concatenate(
            [logits[:, :whole], jnp.where(touched, logits[:, whole:], -1e30)], axis=1
        )
        top = jnp.max(logits, axis=1, keepdims=True)
        expo = jnp.exp(logits - top)
        expo_all[here, :] = expo
        save(expo_all.at[here], expo_ref.at[here])
        ends = jnp.where(owned, expo[:, :128], 0.0)
        total = jnp.sum(jnp.concatenate([ends, expo[:, 128:]], axis=1), axis=1, keepdims=True)
        tops.append(to_row(top, eye))
        sums.append(to_row(top + jnp.log(total), eye))
    join = span // step

    def blocks_of(own):
        return jnp.concatenate(
            [jnp.concatenate(own[k : k + join], axis=1) for k in range(0, len(own), join)], axis=0
        )

    top_ref[...] = blocks_of(tops)
    stats = blocks_of(sums)
    for device in range(stat_ref.shape[0]):
        stat_ref[device] = stats
    for copy in copies:
        copy.wait()


def call_logits(me, shift, table, gathered, picks, embed_here, devices):
    count, width = table.shape
    pieces = [(part, piece, masks) for part, own in enumerate(gathered) for piece, masks in own]
    plan = tuple((part, tuple(masks)) for part, _, masks in pieces)
    block = pieces[0][1].shape[1]
    rows = devices * picks
    span = rows // 8
    vmem = pl.BlockSpec(memory_space=pltpu.VMEM)
    smem = pl.BlockSpec(memory_space=pltpu.SMEM)
    hbm = pl.BlockSpec(memory_space=pl.ANY)
    low, full = jnp.bfloat16, jnp.float32
    return pl.pallas_call(
        functools.partial(logits_kernel, plan, embed_here, picks, span),
        out_shape=[
            jax.ShapeDtypeStruct((devices, block, width), low),
            jax.ShapeDtypeStruct((rows, count), full),
            jax.ShapeDtypeStruct((devices, 8, span), full),
            jax.ShapeDtypeStruct((8, span), full),
        ],
        in_specs=[smem, smem, vmem] + [hbm] * len(pieces),
        out_specs=[hbm, hbm, vmem, vmem],
        scratch_shapes=[
            pltpu.VMEM((devices, block, width), low),
            pltpu.VMEM((rows, count), full),
            pltpu.SemaphoreType.DMA,
            pltpu.SemaphoreType.DMA((devices // 4 + 1,)),
        ],
        compiler_params=pltpu.CompilerParams(vmem_limit_bytes=58 * 2**20),
        cost_estimate=pl.CostEstimate(
            flops=2 * rows * count * width, bytes_accessed=16 * 2**20, transcendentals=0
        ),
    )(me, shift, table, *[piece for _, piece, _ in pieces])


def terms_kernel(plan, picks, me_ref, *refs):
    stat_ref, top_ref, expo_ref, owned_ref, label_ref, scale_ref = refs[:6]
    sinks = refs[6:15]
    terms, out_sem = refs[15:]
    span, count = expo_ref.shape
    width = owned_ref.shape[1]
    chunks = terms.shape[0]
    group = span // picks
    me = me_ref[0]
    step = pl.program_id(0)
    chunk = step ^ lax.div(me, group)
    scales = []
    for half in range(2):
        row = 2 * chunk + half
        sums = stat_ref[:, pl.ds(row, 1), :]
        top = jnp.max(sums, axis=0)
        whole = top + jnp.log(jnp.sum(jnp.exp(sums - top[None]), axis=0))
        scales.append(jnp.exp(top_ref[pl.ds(row, 1), :] - whole))
    scale = jnp.concatenate(scales, axis=1)
    used = label_ref[1:2, :]
    scale = scale * used
    scale_ref[...] = jnp.broadcast_to(scale, scale_ref.shape)
    label = jnp.where(used > 0, label_ref[0:1, :], -1.0)
    eye = eye_mask()
    part = span // 2
    lane = lax.broadcasted_iota(jnp.int32, (part, count), 1)
    for k in range(0, span, part):
        here = slice(k, k + part)
        probs = expo_ref[here, :] * to_column(scale[:, here], eye)
        hot = lane == to_column(label[:, here], eye).astype(jnp.int32)
        d_logits = jnp.where(hot, probs - 1.0, probs).astype(jnp.bfloat16)
        terms[step, here, :] = dot_nn(d_logits, owned_ref[...]).astype(jnp.bfloat16)
    cut = width // 3
    half = sinks[0].shape[0]

    def send(now):
        for b in range(group):
            row = pl.multiple_of((b ^ lax.rem(me, group)) * picks, 16)
            for part, bits in enumerate(plan):
                relative = now * group + b
                spot = sum(
                    1 << (len(bits) - 1 - k) for k, bit in enumerate(bits) if relative & bit
                )
                kind = 0 if spot < half else (2 if spot < half + half // 2 else 1)
                spot = spot - (0, half + half // 2, half)[kind]
                pltpu.make_async_copy(
                    terms.at[now, pl.ds(row, picks), part * cut : (part + 1) * cut],
                    sinks[3 * part + kind].at[spot],
                    out_sem,
                ).start()

    for now in range(chunks):
        pl.when(step == now)(functools.partial(send, now))

    @pl.when(step == chunks - 1)
    def _():
        wait_sinks(sinks, out_sem)


def call_terms(me, stats, tops, expo, owned, labels, plan, picks):
    rows, count = expo.shape
    width = owned.shape[1]
    devices = stats.shape[0]
    span = 2 * stats.shape[2]
    hbm = pl.BlockSpec(memory_space=pl.ANY)
    low = jnp.bfloat16
    group = span // picks

    def tile(lanes):
        return pl.BlockSpec((span, lanes), lambda k, me: (k ^ lax.div(me[0], group), 0))

    row_tile = pl.BlockSpec((8, span), lambda k, me: (0, k ^ lax.div(me[0], group)))
    return pl.pallas_call(
        functools.partial(terms_kernel, plan, picks),
        grid_spec=pltpu.PrefetchScalarGridSpec(
            num_scalar_prefetch=1,
            grid=(rows // span,),
            in_specs=[
                pl.BlockSpec(stats.shape, lambda k, me: (0, 0, 0)),
                pl.BlockSpec(tops.shape, lambda k, me: (0, 0)),
                tile(count),
                pl.BlockSpec(owned.shape, lambda k, me: (0, 0)),
                row_tile,
            ],
            out_specs=[row_tile] + [hbm] * 9,
            scratch_shapes=[
                pltpu.VMEM((rows // span, span, width), low),
                pltpu.SemaphoreType.DMA,
            ],
        ),
        out_shape=[jax.ShapeDtypeStruct((8, rows), jnp.float32)]
        + sink_shapes(devices, (picks, width // 3), low),
        compiler_params=pltpu.CompilerParams(vmem_limit_bytes=48 * 2**20),
        cost_estimate=pl.CostEstimate(
            flops=2 * rows * count * width, bytes_accessed=12 * 2**20, transcendentals=0
        ),
    )(me, stats, tops, expo, owned, labels)


def embed_kernel(picks, shift_ref, expo_ref, scale_ref, label_ref, picked_ref, out_ref, wide, turn):
    here, width = out_ref.shape
    rows, count = expo_ref.shape
    shift = shift_ref[0]
    chunk = pl.program_id(0)

    @pl.when(chunk == 0)
    def _():
        turn[...] = turn_lanes(shift, width)

    eye = eye_mask()
    probs = expo_ref[...] * to_column(scale_ref[0:1, :], eye)
    lane = lax.broadcasted_iota(jnp.int32, (rows, count), 1)
    used = label_ref[1:2, :]
    label = jnp.where(used > 0, label_ref[0:1, :], -1.0)
    hot = lane == to_column(label, eye).astype(jnp.int32)
    terms = jnp.where(hot, probs - 1.0, probs).astype(jnp.bfloat16)
    picked = jnp.concatenate([picked_ref[d, :picks, :] for d in range(rows // picks)], axis=0)
    turned = contract_cols(picked, turn[...]).astype(jnp.bfloat16)
    total = contract_rows(terms, turned)

    @pl.when(chunk == 0)
    def _():
        wide[...] = total

    @pl.when(chunk > 0)
    def _():
        wide[...] = wide[...] + total

    @pl.when(chunk == pl.num_programs(0) - 1)
    def _():
        lane = lax.broadcasted_iota(jnp.int32, (here, width), 1)
        out_ref[...] = jnp.where(lane < width - shift, wide[:here, :], wide[1 : here + 1, :])


def call_embed(shift, expo, scale, labels, picked, picks, here):
    rows, count = expo.shape
    devices, block, width = picked.shape
    smem = pl.BlockSpec(memory_space=pltpu.SMEM)
    step = rows // 8
    row_tile = pl.BlockSpec((8, step), lambda k: (0, k))
    return pl.pallas_call(
        functools.partial(embed_kernel, picks),
        grid=(8,),
        out_shape=jax.ShapeDtypeStruct((here, width), jnp.float32),
        in_specs=[
            smem,
            pl.BlockSpec((step, count), lambda k: (k, 0)),
            row_tile,
            row_tile,
            pl.BlockSpec((devices // 8, block, width), lambda k: (k, 0, 0)),
        ],
        out_specs=pl.BlockSpec((here, width), lambda k: (0, 0)),
        scratch_shapes=[
            pltpu.VMEM((count, width), jnp.float32),
            pltpu.VMEM((width, width), jnp.bfloat16),
        ],
        compiler_params=pltpu.CompilerParams(vmem_limit_bytes=58 * 2**20),
        cost_estimate=pl.CostEstimate(
            flops=16 * rows * count * width, bytes_accessed=64 * 2**20, transcendentals=0
        ),
    )(shift, expo, scale, labels, picked)


def step_kernel(counts, *refs):
    weight_ref, first_ref, second_ref = refs[:3]
    grad_ref, step_ref = refs[-2:]
    start, row = 3, 0
    width = refs[3].shape[2]
    share = width // 128
    for count in counts:
        total = add_terms([ref[0] for ref in refs[start : start + count]])
        rows = total.shape[0]
        for q in range(share):
            grad_ref[pl.ds(share * row + q, rows, stride=share), :] = total[
                :, 128 * q : 128 * q + 128
            ]
        start, row = start + count, row + rows
    step_ref[...] = adam_step(
        weight_ref[...], grad_ref[...], first_ref[...], second_ref[...], float(ADAM_STEP), decay_rate
    )


def call_step(weight, first, second, terms):
    shape = jax.ShapeDtypeStruct((weight.shape[0] // 128, 128), jnp.float32)
    vmem = pl.BlockSpec(memory_space=pltpu.VMEM)
    given = [value.reshape(shape.shape) for value in (weight, first, second)]
    blocks = [term for own in terms for term in own]
    first_block = pl.BlockSpec((1,) + blocks[0].shape[1:], lambda k: (0, 0, 0))
    grad, step = pl.pallas_call(
        functools.partial(step_kernel, [len(own) for own in terms]),
        grid=(1,),
        out_shape=[shape] * 2,
        in_specs=[vmem] * 3 + [first_block] * len(blocks),
        out_specs=[vmem] * 2,
        compiler_params=pltpu.CompilerParams(vmem_limit_bytes=24 * 2**20),
    )(*given, *blocks)
    return grad.reshape(-1), step.reshape(-1)


def plain_forward(mats_all, vecs_all, block_input, span_lengths):
    seq_here, length, width = block_input.shape
    rows_here = seq_here * length
    heads_count = width // HEAD_DIM
    head_scale = HEAD_DIM ** (-0.5)
    low = jnp.bfloat16
    w_qkv, w_out, w_up, w_down = split_mats(mats_all)
    bias_q, bias_v, bias_out, gain_one, shift_one, bias_up, bias_down, gain_two, shift_two = (
        split_vecs(vecs_all)
    )
    valid = jnp.arange(length)[None, :] < span_lengths[:, None]
    valid_col = valid.reshape(rows_here, 1).astype(jnp.float32)
    tok_rows = (block_input * valid[:, :, None].astype(low)).reshape(rows_here, width)
    qkv_bias = jnp.concatenate([bias_q, jnp.zeros((width,), jnp.float32), bias_v])
    projected = (jnp.dot(tok_rows, w_qkv, preferred_element_type=jnp.float32) + qkv_bias).astype(
        low
    )
    shaped = projected.reshape(seq_here, length, 3, heads_count, HEAD_DIM)
    queries = shaped[:, :, 0]
    key_rows = shaped[:, :, 1]
    value_rows = shaped[:, :, 2]
    key_valid = valid[:, None, None, :]

    def make_scores():
        raw = (
            jnp.einsum("sqhd,skhd->shqk", queries, key_rows, preferred_element_type=jnp.float32)
            * head_scale
        )
        return jnp.where(key_valid, raw, -1e30)

    scores = make_scores()
    row_max = jnp.max(scores, axis=-1, keepdims=True)
    expo_vals = jnp.exp(scores - row_max)
    row_sum = jnp.sum(expo_vals, axis=-1, keepdims=True)
    row_lse = row_max + jnp.log(row_sum)
    attn_probs = (expo_vals / row_sum).astype(low)
    attended = (
        jnp.einsum("shqk,skhd->sqhd", attn_probs, value_rows, preferred_element_type=jnp.float32)
        .reshape(rows_here, width)
        .astype(low)
    )
    branch = jnp.dot(attended, w_out, preferred_element_type=jnp.float32) + bias_out
    normed_one, inverse_one = center_scale(tok_rows.astype(jnp.float32) + branch)
    hidden_one = normed_one * gain_one + shift_one
    hidden_low = hidden_one.astype(low)
    pre_act = jnp.dot(hidden_low, w_up, preferred_element_type=jnp.float32) + bias_up
    act_low = jax.nn.gelu(pre_act, approximate=False).astype(low)
    ffn_out = jnp.dot(act_low, w_down, preferred_element_type=jnp.float32) + bias_down
    normed_two, inverse_two = center_scale(hidden_one + ffn_out)
    output = (normed_two * gain_two + shift_two) * valid_col

    def plain_backward(d_output):
        d_gain_two = jnp.sum(d_output * normed_two, axis=0)
        d_shift_two = jnp.sum(d_output, axis=0)
        d_resid_two = norm_back(d_output * gain_two, normed_two, inverse_two)
        d_ffn = d_resid_two.astype(low)
        d_bias_down = jnp.sum(d_ffn.astype(jnp.float32), axis=0)
        d_w_down = contract_rows(act_low, d_ffn)
        d_act = contract_cols(d_ffn, w_down)
        d_pre = (d_act * gelu_slope(pre_act)).astype(low)
        d_bias_up = jnp.sum(d_pre.astype(jnp.float32), axis=0)
        d_w_up = contract_rows(hidden_low, d_pre)
        d_hidden = contract_cols(d_pre, w_up) + d_resid_two
        d_gain_one = jnp.sum(d_hidden * normed_one, axis=0)
        d_shift_one = jnp.sum(d_hidden, axis=0)
        d_resid_one = norm_back(d_hidden * gain_one, normed_one, inverse_one)
        d_branch = d_resid_one.astype(low)
        d_bias_out = jnp.sum(d_branch.astype(jnp.float32), axis=0)
        d_w_out = contract_rows(attended, d_branch)
        d_attended = (
            contract_cols(d_branch, w_out).astype(low).reshape(seq_here, length, heads_count, HEAD_DIM)
        )
        probs_again = jnp.exp(make_scores() - row_lse)
        probs_low = probs_again.astype(low)
        d_probs = jnp.einsum(
            "sqhd,skhd->shqk", d_attended, value_rows, preferred_element_type=jnp.float32
        )
        d_values = jnp.einsum(
            "shqk,sqhd->skhd", probs_low, d_attended, preferred_element_type=jnp.float32
        )
        row_delta = jnp.sum(d_probs * probs_again, axis=-1, keepdims=True)
        d_scores = (probs_again * (d_probs - row_delta)).astype(low)
        d_queries = (
            jnp.einsum("shqk,skhd->sqhd", d_scores, key_rows, preferred_element_type=jnp.float32)
            * head_scale
        )
        d_keys = (
            jnp.einsum("shqk,sqhd->skhd", d_scores, queries, preferred_element_type=jnp.float32)
            * head_scale
        )
        d_qkv = jnp.concatenate(
            [
                d_queries.reshape(rows_here, width),
                d_keys.reshape(rows_here, width),
                d_values.reshape(rows_here, width),
            ],
            axis=1,
        ).astype(low)
        d_qkv_float = d_qkv.astype(jnp.float32)
        d_bias_q = jnp.sum(d_qkv_float[:, :width], axis=0)
        d_bias_v = jnp.sum(d_qkv_float[:, 2 * width :], axis=0)
        d_w_qkv = contract_rows(tok_rows, d_qkv)
        grad_input = ((contract_cols(d_qkv, w_qkv) + d_resid_one) * valid_col).reshape(
            seq_here, length, width
        )
        d_mats = jnp.concatenate(
            [
                piece.astype(low).reshape(-1, width)
                for piece in (d_w_qkv, d_w_out, d_w_up, d_w_down)
            ]
        )
        d_vecs = jnp.concatenate(
            [
                d_bias_q,
                d_bias_v,
                d_bias_out,
                d_gain_one,
                d_shift_one,
                d_bias_up,
                d_bias_down,
                d_gain_two,
                d_shift_two,
            ]
        )
        return grad_input, d_mats, d_vecs

    return output, plain_backward


def on_device(
    names,
    core,
    block_input,
    span_lengths,
    mlm_positions,
    mlm_labels,
    span_pairs,
    layer_mats,
    vectors,
    embedding,
    mom1_mats,
    mom2_mats,
    mom1_vecs,
    mom2_vecs,
    mom1_embed,
    mom2_embed,
):
    seq_here, length, width = block_input.shape
    rows_here = seq_here * length
    devices = 2 ** len(names)
    me = lax.axis_index(names)
    orders = bit_orders(names, core)
    slots = mlm_positions.shape[1]
    picks_here = seq_here * slots
    low = jnp.bfloat16

    third = layer_mats.shape[0] // width // 3
    by_kernel = third % 16 == 0
    vec_here = vectors.shape[0]
    mats_low = layer_mats.astype(low).reshape(3, third, width)

    labels_flat = mlm_labels.reshape(-1)
    common = jnp.concatenate(
        [
            value.astype(low)
            for value in (
                vectors,
                labels_flat // 256,
                labels_flat % 256,
                span_pairs // 256,
                span_pairs % 256,
                span_lengths // 4,
            )
        ]
    )
    sizes = [vec_here, picks_here, picks_here, seq_here, seq_here, seq_here]
    common = jnp.pad(common, (0, width - common.shape[0]))
    others = jnp.arange(devices)[:, None]
    right, left = (me + 1) % devices, (me + devices - 1) % devices
    border = jnp.where(
        others == right,
        embedding[-width:].astype(low),
        jnp.where(others == left, embedding[:width].astype(low), jnp.zeros((), low)),
    )
    small = jnp.stack([jnp.broadcast_to(common, border.shape), border], axis=1)

    def share(small):
        return lax.all_to_all(small, names, 0, 0, tiled=True)

    embed_here = embedding.shape[0]
    shifted_rows = -(-embed_here // width)
    over = shifted_rows * width - embed_here
    shift = (me * (embed_here % width)) % width
    first_row = me * (embed_here // width) + (me * (embed_here % width)) // width

    def table_shard(embedding):
        return jnp.pad(embedding.astype(low), (0, over)).reshape(shifted_rows, width)


    def unpack(small_all):
        starts = [sum(sizes[:k]) for k in range(len(sizes))]
        vecs_all, labels_high, labels_low, pairs_high, pairs_low, quarter_all = (
            small_all[:, 0, start : start + size] for start, size in zip(starts, sizes)
        )
        vec_rows = vecs_all.reshape(-1).astype(jnp.float32).reshape(-1, width)

        def whole(high, small):
            return (high.astype(jnp.int32) * 256 + small.astype(jnp.int32)).reshape(-1)

        quarter_all = quarter_all.astype(jnp.int32).reshape(-1)
        used = (jnp.arange(slots)[None, :] < quarter_all[:, None]).reshape(-1)
        row_of = whole(labels_high, labels_low) - first_row
        from_left = lax.dynamic_index_in_dim(small_all[:, 1], left, 0, False)
        from_right = lax.dynamic_index_in_dim(small_all[:, 1], right, 0, False)
        right_rows = jnp.pad(from_right, (width - over, over)).reshape(2, width)
        return vec_rows, row_of, used, whole(pairs_high, pairs_low), from_left, right_rows

    seq_start = jnp.arange(seq_here, dtype=jnp.int32) * length

    def span_terms(cls_all, pairs_all):
        span_scale = 2.0 / math.sqrt(width)
        columns = jnp.arange(cls_all.shape[0])
        sims = contract_cols(cls_all, cls_all) * span_scale
        sims = jnp.where(columns[None, :] == columns[:, None], -1e30, sims)
        partner_hot = (columns[None, :] == pairs_all[:, None]).astype(jnp.float32)
        d_sims = (jax.nn.softmax(sims, axis=-1) - partner_hot).astype(low)
        mine = me * seq_here
        d_sims_rows = lax.dynamic_slice_in_dim(d_sims, mine, seq_here, 0)
        d_sims_cols = lax.dynamic_slice_in_dim(d_sims, mine, seq_here, 1)
        return (
            jnp.dot(d_sims_rows, cls_all, preferred_element_type=jnp.float32)
            + contract_rows(d_sims_cols, cls_all)
        ) * span_scale

    step_float = float(ADAM_STEP)

    def embed_step(grad_rows):
        grad = grad_rows.reshape(-1)[:embed_here]
        return grad, adam_step(embedding, grad, mom1_embed, mom2_embed, step_float, decay_rate)

    def vector_terms(d_vecs):
        return lax.all_to_all(d_vecs.reshape(devices, 1, vec_here), names, 0, 0, tiled=True)

    cut = width // 3
    columns = [slice(k * cut, (k + 1) * cut) for k in range(3)]
    back_orders = [order[::-1] for order in orders]
    if by_kernel:
        lone = me.astype(jnp.int32).reshape(1)
        lone_shift = shift.astype(jnp.int32).reshape(1)
        tok_rows = block_input.reshape(rows_here, width)
        relative = jnp.arange(devices, dtype=jnp.int32) ^ me.astype(jnp.int32)
        spots = jnp.stack(
            [
                sum(
                    ((relative & device_mask(name, names)) != 0).astype(jnp.int32)
                    << (len(names) - 1 - k)
                    for k, name in enumerate(order)
                )
                for order in back_orders
            ],
            axis=1,
        ).reshape(-1)
        places = jnp.concatenate(
            [
                (mlm_positions + seq_start[:, None]).reshape(-1),
                seq_start,
                jnp.full((16 - seq_here,), -1, jnp.int32),
            ]
        )
        table_rows = -(-(shifted_rows + 1) // 128) * 128

        def prepare(embedding, small_all):
            vec_rows, row_of, used, pairs_all, from_left, right_rows = unpack(small_all)
            ends = jnp.pad(
                jnp.concatenate([from_left[None], right_rows]).astype(jnp.float32),
                ((0, 5), (0, 0)),
            )
            labels = jnp.pad(
                jnp.stack([row_of.astype(jnp.float32), used.astype(jnp.float32)]),
                ((0, 6), (0, 0)),
            )
            shifted = table_shard(embedding)
            table, owned = call_table(lone_shift, shifted, ends, table_rows, embed_here)
            return table, owned, labels, vec_rows, pairs_all

        gathered, (table, owned, labels, vec_rows, pairs_all) = gather_relative(
            mats_low[:, None], orders, names, (embedding, small), share, prepare
        )
        *heads, saved = call_forward(
            lone, span_lengths, places[None], tok_rows, vec_rows, gathered, devices, seq_here
        )
        heads_all, _ = gather_relative(heads, orders, names)
        picked, expo, stats, tops = call_logits(
            lone, lone_shift, table, heads_all, picks_here, embed_here, devices
        )
        stats = lax.all_to_all(stats, names, 0, 0, tiled=True)
        plan = tuple(tuple(device_mask(name, names) for name in order) for order in back_orders)
        scale, *sinks = call_terms(
            lone, stats, tops, expo, owned, labels, plan, picks_here
        )
        d_cls = span_terms(
            picked[:, picks_here : picks_here + seq_here].reshape(-1, width), pairs_all
        )
        d_parts, _ = reduce_relative(
            sinks[0::3], list(zip(sinks[1::3], sinks[2::3])), back_orders
        )
        d_parts = [add_terms([term[0] for term in terms]) for terms in d_parts]
        top = jnp.concatenate(
            [jnp.concatenate(d_parts, axis=1), jnp.pad(d_cls, ((0, 16 - seq_here), (0, 0)))]
        )
        grad_input, d_vecs, *sinks = call_backward(
            span_lengths, spots, places[None], tok_rows, vec_rows, top, saved, third, seq_here
        )
        grad_input = grad_input.reshape(seq_here, length, width)
        def table_grad(state):
            expo, picked, d_vecs = state
            grad_embed = call_embed(
                lone_shift, expo, scale, labels, picked, picks_here, shifted_rows
            )
            grad_embed, d_vecs = lax.optimization_barrier((grad_embed, d_vecs))
            return grad_embed, vector_terms(d_vecs)

        def table_step(state):
            grad_embed, terms = state
            return *embed_step(grad_embed), jnp.sum(terms, axis=(0, 1))

        terms, (grad_embed, step_embed, grad_vecs) = reduce_relative(
            sinks[0::3],
            list(zip(sinks[1::3], sinks[2::3])),
            back_orders,
            (expo, picked, d_vecs),
            {0: table_grad, len(names) - 2: table_step},
            1,
        )
        grad_mats, step_mats = call_step(layer_mats, mom1_mats, mom2_mats, terms)
    else:
        vec_rows, row_of, used, pairs_all, from_left, right_rows = unpack(share(small))
        same_row = (jnp.arange(width) < width - shift)[None, :]
        tall = jnp.concatenate(
            [from_left[None], table_shard(embedding), jnp.zeros((1, width), low)]
        )
        tall = tall.at[shifted_rows : shifted_rows + 2].add(right_rows)
        lanes = jnp.arange(width)
        turn = ((lanes[:, None] + shift) % width == lanes[None, :]).astype(low)
        rolled = jnp.where(same_row, tall[1:], tall[:-1])
        table = jnp.dot(rolled, turn, preferred_element_type=jnp.float32).astype(low)
        row_start = jnp.arange(shifted_rows + 1) * width - shift
        owned = (row_start >= 0) & (row_start < embed_here)
        touched = (row_start + width > 0) & (row_start < embed_here)
        gathered = [gather_bits(mats_low[k], orders[k], names) for k in range(3)]
        mats_all = jnp.stack(gathered, axis=1).reshape(-1)
        output, plain_backward = plain_forward(
            mats_all, vec_rows.reshape(-1), block_input, span_lengths
        )
        output_seq = output.reshape(seq_here, length, width)
        picked_here = jnp.take_along_axis(output_seq, mlm_positions[:, :, None], axis=1)
        heads = jnp.concatenate([picked_here.reshape(-1, width), output_seq[:, 0, :]]).astype(low)
        heads_all = jnp.concatenate(
            [gather_bits(heads[:, c], order, names) for c, order in zip(columns, orders)], axis=2
        )
        picked = heads_all[:, :picks_here, :].reshape(-1, width)
        logits = contract_cols(picked, table)
        masked = jnp.where(owned[None, :], logits, -jnp.inf)
        part_max = jnp.max(masked, axis=-1)
        part_sum = jnp.sum(jnp.exp(masked - part_max[:, None]), axis=-1)
        full_max = lax.pmax(part_max, names)
        full_sum = lax.psum(part_sum * jnp.exp(part_max - full_max), names)
        hot = row_of[:, None] == jnp.arange(shifted_rows + 1)[None, :]
        probs = jnp.exp(logits - full_max[:, None]) / full_sum[:, None]
        d_logits = jnp.where(
            used[:, None] & touched[None, :], probs - hot.astype(jnp.float32), 0.0
        ).astype(low)
        d_picked = jnp.dot(
            d_logits, jnp.where(owned[:, None], table, 0), preferred_element_type=jnp.float32
        )
        blocks = d_picked.astype(low).reshape(devices, picks_here, width)
        d_picked = jnp.concatenate(
            [
                reduce_bits(blocks[:, :, c], order, names)
                for c, order in zip(columns, back_orders)
            ],
            axis=1,
        ).astype(jnp.float32)
        select = (mlm_positions[:, :, None] == jnp.arange(length)[None, None, :]).astype(
            jnp.float32
        )
        d_output_seq = jnp.einsum(
            "gor,gon->grn",
            select,
            d_picked.reshape(seq_here, slots, width),
            precision=lax.Precision.HIGHEST,
        )
        d_cls = span_terms(heads_all[:, picks_here:, :].reshape(-1, width), pairs_all)
        d_output_seq = d_output_seq.at[:, 0, :].add(d_cls)
        valid = jnp.arange(length)[None, :] < span_lengths[:, None]
        d_output = d_output_seq.reshape(rows_here, width) * valid.reshape(rows_here, 1)
        grad_input, d_mats, d_vecs = plain_backward(d_output)
        d_mats = d_mats.reshape(devices, 3, third, width)
        summed = [
            reduce_bits(d_mats[:, k], back_orders[k], names).astype(jnp.float32) for k in range(3)
        ]
        picked_turned = jnp.dot(picked, turn.T, preferred_element_type=jnp.float32).astype(low)
        d_rolled = contract_rows(d_logits, picked_turned)
        grad_embed, step_embed = embed_step(jnp.where(same_row, d_rolled[:-1], d_rolled[1:]))
        grad_vecs = jnp.sum(vector_terms(d_vecs), axis=(0, 1))
        grad_mats = jnp.concatenate(summed).reshape(-1)
        step_mats = adam_step(layer_mats, grad_mats, mom1_mats, mom2_mats, step_float, decay_rate)
    step_vecs = adam_step(vectors, grad_vecs, mom1_vecs, mom2_vecs, step_float, 0.0)
    return (grad_input, grad_mats, grad_vecs, grad_embed, step_mats, step_vecs, step_embed)


def solution(mesh):
    fsdp_bits = mesh.shape["fsdp"].bit_length() - 1
    rep_bits = mesh.shape["rep"].bit_length() - 1
    names = tuple(f"f{k}" for k in reversed(range(fsdp_bits)))
    core = names[-1]
    names = names + tuple(f"r{k}" for k in reversed(range(rep_bits)))
    bits = Mesh(mesh.devices.reshape((2,) * len(names)), names)
    seqs = P(names, None, None)
    pairs = P(names, None)
    flat = P(names)
    return jax.shard_map(
        functools.partial(on_device, names, core),
        mesh=bits,
        in_specs=(seqs, flat, pairs, pairs) + (flat,) * 10,
        out_specs=(seqs,) + (flat,) * 6,
        check_vma=False,
    )
```

profile of v0, /device:TPU:0, one launch (start us, length us, event | category | flops | bytes accessed | tf_op | source)
XLA Modules:
  0.0 311.2 jit_solution(18186604777400719218)
XLA Ops:
  0.6 1.4 convert_element_type.605
  2.2 4.1 %collective-permute-start = (bf16[1,96,768]{2,1,0:T(8,128)(2,1)S(1)}, bf16[1,96,768]{2,1,0:T(8,128)(2,1)}, u32[]{:S(2)}, u32[]{:S(2)}) collective-permute-start(bf16[1,96,768]{2,1,0:T(8,128)(2,1)S(1)} %unstack.19), channel_id=1, source_target_pairs={{0,16},{16,0},{1,17},{17,1},{2,18},{18,2},{3,19},{19,3},{4,20},{20... | collective-permute-start | bytes 442376 | tf_op jit(solution)/shard_map/ppermute | solution.py:89
  6.7 3.0 collective-permute-start.6
  10.8 9.8 %collective-permute-done = bf16[1,96,768]{2,1,0:T(8,128)(2,1)} collective-permute-done((bf16[1,96,768]{2,1,0:T(8,128)(2,1)S(1)}, bf16[1,96,768]{2,1,0:T(8,128)(2,1)}, u32[]{:S(2)}, u32[]{:S(2)}) %collective-permute-start) | collective-permute-done | bytes 147488 | tf_op jit(solution)/shard_map/ppermute | solution.py:89
  21.5 1.9 collective-permute-start.1
  24.7 1.9 collective-permute-start.4
  29.0 1.3 collective-permute-start.2
  30.3 3.6 %collective-permute-done.4 = bf16[2,96,768]{2,1,0:T(8,128)(2,1)S(1)} collective-permute-done((bf16[2,96,768]{2,1,0:T(8,128)(2,1)S(1)}, bf16[2,96,768]{2,1,0:T(8,128)(2,1)S(1)}, u32[]{:S(2)}, u32[]{:S(2)}) %collective-permute-start.4) | collective-permute-done | bytes 294944 | tf_op jit(solution)/shard_map/ppermute | solution.py:89
  36.9 1.5 collective-permute-start.8
  38.4 5.8 %all-to-all-start = ((bf16[32,2,768]{2,1,0:T(2,128)(2,1)}), bf16[32,2,768]{2,1,0:T(2,128)(2,1)}, u32[]{:S(2)}, u32[]{:S(2)}) async-start(bf16[32,2,768]{2,1,0:T(2,128)(2,1)} %pad_maximum_fusion.15), calls=%async_computation | async-start | bytes 196608 | tf_op jit(solution)/shard_map/all_to_all | solution.py:1163
  44.9 2.2 pad_maximum_fusion.refs_5_
  47.0 1.8 collective-permute-done.5
  48.9 2.4 pad_maximum_fusion.1.refs_9_
  51.3 1.5 collective-permute-start.12
  54.1 2.4 pad_maximum_fusion.2.refs_13_
  60.3 1.6 collective-permute-start.15
  64.9 1.7 shard_map.189
  68.3 9.0 %collective-permute-done.12.refs_10_ = bf16[8,96,768]{2,1,0:T(8,128)(2,1)} collective-permute-done((bf16[8,96,768]{2,1,0:T(8,128)(2,1)}, bf16[8,96,768]{2,1,0:T(8,128)(2,1)}, u32[]{:S(2)}, u32[]{:S(2)}) %collective-permute-start.12) | collective-permute-done | bytes 1179680 | tf_op jit(solution)/shard_map/ppermute | solution.py:89
  78.6 7.5 %collective-permute-done.15.refs_14_ = bf16[8,96,768]{2,1,0:T(8,128)(2,1)} collective-permute-done((bf16[8,96,768]{2,1,0:T(8,128)(2,1)}, bf16[8,96,768]{2,1,0:T(8,128)(2,1)}, u32[]{:S(2)}, u32[]{:S(2)}) %collective-permute-start.15) | collective-permute-done | bytes 1179680 | tf_op jit(solution)/shard_map/ppermute | solution.py:89
  87.4 1.9 collective-permute-done.11.refs_8_
  89.3 1.7 collective-permute-done.17.refs_16_
  91.0 13.8 %shard_map.190 = (bf16[1,80,256]{2,1,0:T(8,128)(2,1)}, bf16[1,80,256]{2,1,0:T(8,128)(2,1)}, bf16[1,80,256]{2,1,0:T(8,128)(2,1)}, bf16[9216,768]{1,0:T(8,128)(2,1...) custom-call(s32[1]{0:T(128)} %bitcast.4.refs_0_.me_ref, ...), custom_call_target="tpu_custom_call" | custom-call | flops 3623878656 | bytes 50331648 | tf_op jit(solution)/shard_map/pallas_call | solution.py:549
  104.8 3.1 collective-permute-start.18
  108.0 2.8 collective-permute-start.30
  111.6 3.3 %collective-permute-done.30 = bf16[1,80,256]{2,1,0:T(8,128)(2,1)S(1)} collective-permute-done((bf16[1,80,256]{2,1,0:T(8,128)(2,1)}, bf16[1,80,256]{2,1,0:T(8,128)(2,1)S(1)}, u32[]{:S(2)}, u32[]{:S(2)}) %collective-permute-start.30) | collective-permute-done | bytes 40992 | tf_op jit(solution)/shard_map/ppermute | solution.py:89
  120.3 1.9 collective-permute-start.32
  124.5 1.3 collective-permute-done.32
  128.7 2.2 collective-permute-start.21
  131.4 4.8 %collective-permute-done.33.refs_12_ = bf16[8,80,256]{2,1,0:T(8,128)(2,1)} collective-permute-done((bf16[8,80,256]{2,1,0:T(8,128)(2,1)S(1)}, bf16[8,80,256]{2,1,0:T(8,128)(2,1)}, u32[]{:S(2)}, u32[]{:S(2)}) %collective-permute-start.33) | collective-permute-done | bytes 327712 | tf_op jit(solution)/shard_map/ppermute | solution.py:89
  137.0 1.3 collective-permute-done.21.refs_4_
  140.3 9.1 %shard_map.191 = (bf16[32,80,768]{2,1,0:T(8,128)(2,1)}, f32[2048,1024]{1,0:T(8,128)}, f32[32,8,256]{2,1,0:T(8,128)}, f32[8,256]{1,0:T(8,128)}) custom-call(s32[1]{0:T(128)} %bitcast.4.refs_0_.me_ref, s32[1]{0:T(128)} %bitcast.2.shift_ref.refs_1_, bf16[1024,768]{1,0:T(8,128)(2,1)} %copy-done.16, bf16[8,80,256]{2,1,0:T(8,128)(2,1)} %copy-done.28, ...), custom_call_target="tpu_custom_call" | custom-call | flops 3221225472 | bytes 16777216 | tf_op jit(solution)/shard_map/pallas_call | solution.py:754
  149.5 3.3 %all-to-all-start.1 = ((f32[32,8,256]{2,1,0:T(8,128)}), f32[32,8,256]{2,1,0:T(8,128)S(1)}, u32[]{:S(2)}, u32[]{:S(2)}) async-start(f32[32,8,256]{2,1,0:T(8,128)} %get-tuple-element.99), calls=%async_computation.1 | async-start | bytes 524288 | tf_op jit(solution)/shard_map/all_to_all | solution.py:1271
  154.2 9.3 %all-to-all-done.1.refs_0_ = f32[32,8,256]{2,1,0:T(8,128)S(1)} async-done(((f32[32,8,256]{2,1,0:T(8,128)}), f32[32,8,256]{2,1,0:T(8,128)S(1)}, u32[]{:S(2)}, u32[]{:S(2)}) %all-to-all-start.1) | async-done | bytes 262176 | tf_op jit(solution)/shard_map/all_to_all | solution.py:1271
  163.6 8.0 %shard_map.192 = (f32[8,2048]{1,0:T(8,128)S(1)}, bf16[16,64,256]{2,1,0:T(8,128)(2,1)S(1)}, bf16[8,64,256]{2,1,0:T(8,128)(2,1)S(1)}, bf16[8,64,256]{2,1,0:T(8,128...) custom-call(s32[1]{0:T(128)} %bitcast.4.refs_0_.me_ref, ...), custom_call_target="tpu_custom_call" | custom-call | flops 3221225472 | bytes 12582912 | tf_op jit(solution)/shard_map/pallas_call | solution.py:849
  177.0 5.0 %collective-permute-done.38 = bf16[8,64,256]{2,1,0:T(8,128)(2,1)S(1)} collective-permute-done((bf16[8,64,256]{2,1,0:T(8,128)(2,1)S(1)}, bf16[8,64,256]{2,1,0:T(8,128)(2,1)S(1)}, u32[]{:S(2)}, u32[]{:S(2)}) %collective-permute-start.38) | collective-permute-done | bytes 262176 | tf_op jit(solution)/shard_map/ppermute | solution.py:89
  184.4 1.7 collective-permute-start.51
  190.2 1.4 collective-permute-start.52
  193.0 1.7 collective-permute-start.47
  198.3 1.5 collective-permute-done.53
  200.6 21.2 %shard_map.193 = (f32[256,768]{1,0:T(8,128)}, f32[12,768]{1,0:T(8,128)}, bf16[16,96,768]{2,1,0:T(8,128)(2,1)}, bf16[8,96,768]{2,1,0:T(8,128)(2,1)}, bf16[8,96,76...) custom-call(s32[2]{0:T(128)} %refs_0_.1, ...), custom_call_target="tpu_custom_call" | custom-call | flops 7247757312 | bytes 50331648 | tf_op jit(solution)/shard_map/pallas_call | solution.py:588
  223.0 2.0 collective-permute-done.55
  225.1 2.7 add_convert_fusion.2
  228.3 1.6 collective-permute-start.56
  230.0 1.4 add_convert_fusion.1
  231.7 2.0 collective-permute-start.62
  235.0 14.9 %shard_map.194 = f32[954,768]{1,0:T(8,128)} custom-call(s32[1]{0:T(128)} %bitcast.2.shift_ref.refs_1_, f32[2048,1024]{1,0:T(8,128)} %get-tuple-element.146.refs_2_.expo_ref, f32[8,2048]{1,0:T(8,128)} %copy-done.17, f32[8,2048]{1,0:T(8,128)} %copy-done.15, bf16[32,80,768]{2,1,0:T(8,128)(2,1)} %get-tuple-element.148.picked_ref), custom_call_target="tpu_custom_call" | custom-call | flops 25769803776 | bytes 67108864 | tf_op jit(solution)/shard_map/pallas_call | solution.py:917
  249.9 1.5 reshape.465
  251.4 3.4 %all-to-all-start.2 = ((f32[32,1,288]{2,1,0:T(1,128)}), f32[32,1,288]{2,1,0:T(1,128)}, u32[]{:S(2)}, u32[]{:S(2)}) async-start(f32[32,1,288]{2,1,0:T(1,128)} %reshape.465), calls=%async_computation.2 | async-start | bytes 98304 | tf_op jit(solution)/shard_map/all_to_all | solution.py:1217
  254.8 1.8 collective-permute-done.56
  256.6 1.6 add_convert_fusion.5
  260.6 1.5 add_convert_fusion.4
  262.1 1.6 collective-permute-start.63
  263.7 1.5 add_convert_fusion.3
  266.3 1.4 convert_add_fusion.2.refs_3_
  267.7 1.4 convert_add_fusion.1.refs_7_
  269.1 1.6 convert_add_fusion.refs_11_
  270.8 4.2 %collective-permute-done.57.refs_4_ = bf16[4,96,768]{2,1,0:T(8,128)(2,1)S(1)} collective-permute-done((bf16[4,96,768]{2,1,0:T(8,128)(2,1)S(1)}, bf16[4,96,768]{2,1,0:T(8,128)(2,1)S(1)}, u32[]{:S(2)}, u32[]{:S(2)}) %collective-permute-start.57) | collective-permute-done | bytes 589856 | tf_op jit(solution)/shard_map/ppermute | solution.py:89
  275.0 1.6 collective-permute-start.58
  277.4 4.0 %collective-permute-done.69.refs_12_ = bf16[4,96,768]{2,1,0:T(8,128)(2,1)S(1)} collective-permute-done((bf16[4,96,768]{2,1,0:T(8,128)(2,1)S(1)}, bf16[4,96,768]{2,1,0:T(8,128)(2,1)S(1)}, u32[]{:S(2)}, u32[]{:S(2)}) %collective-permute-start.69) | collective-permute-done | bytes 589856 | tf_op jit(solution)/shard_map/ppermute | solution.py:89
  282.0 3.6 %collective-permute-done.58.refs_5_ = bf16[2,96,768]{2,1,0:T(8,128)(2,1)S(1)} collective-permute-done((bf16[2,96,768]{2,1,0:T(8,128)(2,1)S(1)}, bf16[2,96,768]{2,1,0:T(8,128)(2,1)S(1)}, u32[]{:S(2)}, u32[]{:S(2)}) %collective-permute-start.58) | collective-permute-done | bytes 294944 | tf_op jit(solution)/shard_map/ppermute | solution.py:89
  288.3 1.8 collective-permute-start.65
  292.7 4.1 %reshape.447 = f32[732672]{0:T(1024)} reshape(f32[954,768]{1,0:T(8,128)} %shard_map.194) | data formatting | bytes 5861376 | tf_op jit(solution)/shard_map/reshape | solution.py:1213
  297.7 9.0 %fusion.5 = (f32[732528]{0:T(1024)}, f32[732528]{0:T(1024)}) fusion(f32[732528]{0:T(1024)} %param.21, f32[732528]{0:T(1024)} %param.27, f32[732528]{0:T(1024)} %param.26, f32[732672]{0:T(1024)} %reshape.447), kind=kLoop, calls=%fused_computation.6 | loop fusion | flops 9522864 | bytes 17580672 | tf_op jit(solution)/shard_map/add | solution.py:85
  307.5 3.5 %shard_map.195 = (f32[1728,128]{1,0:T(8,128)}, f32[1728,128]{1,0:T(8,128)}) custom-call(f32[1728,128]{1,0:T(8,128)S(1)} %bitcast.25, f32[1728,128]{1,0:T(8,128)S(1)} %bitcast.26, f32[1728,128]{1,0:T(8,128)S(1)} %bitcast.27, f32[4,96,768]{2,1,0:T(8,128)S(1)} %convert_add_fusion.2.refs_3_, bf16[4,96,768]{2,1,0:T(8,128)(2,1)S(1)} %copy-done.2, ...), custom_call_target="tpu_custom_call" | custom-call | tf_op jit(solution)/shard_map/pallas_call | solution.py:965
  (276 shorter events, 70.7 us)
Async XLA Ops:
  2.2 18.4 %collective-permute-start = (bf16[1,96,768]{2,1,0:T(8,128)(2,1)S(1)}, bf16[1,96,768]{2,1,0:T(8,128)(2,1)}, u32[]{:S(2)}, u32[]{:S(2)}) collective-permute-start(bf16[1,96,768]{2,1,0:T(8,128)(2,1)S(1)} %unstack.19), channel_id=1, source_target_pairs={{0,16},{16,0},{1,17},{17,1},{2,18},{18,2},{3,19},{19,3},{4,20},{20... | collective-permute-start | bytes 442376 | tf_op jit(solution)/shard_map/ppermute | solution.py:89
  6.5 17.3 %collective-permute-start.3 = (bf16[1,96,768]{2,1,0:T(8,128)(2,1)S(1)}, bf16[1,96,768]{2,1,0:T(8,128)(2,1)}, u32[]{:S(2)}, u32[]{:S(2)}) collective-permute-start(bf16[1,96,768]{2,1,0:T(8,128)(2,1)S(1)} %unstack.21), channel_id=1, source_target_pairs={{0,16},{16,0},{1,17},{17,1},{2,18},{18,2},{3,19},{19,3},{4,20},{20... | collective-permute-start | bytes 442376 | tf_op jit(solution)/shard_map/ppermute | solution.py:89
  6.7 20.8 %collective-permute-start.6 = (bf16[1,96,768]{2,1,0:T(8,128)(2,1)S(1)}, bf16[1,96,768]{2,1,0:T(8,128)(2,1)}, u32[]{:S(2)}, u32[]{:S(2)}) collective-permute-start(bf16[1,96,768]{2,1,0:T(8,128)(2,1)S(1)} %unstack.23), channel_id=1, source_target_pairs={{0,16},{16,0},{1,17},{17,1},{2,18},{18,2},{3,19},{19,3},{4,20},{20... | collective-permute-start | bytes 442376 | tf_op jit(solution)/shard_map/ppermute | solution.py:89
  21.5 7.4 %collective-permute-start.1 = (bf16[2,96,768]{2,1,0:T(8,128)(2,1)S(1)}, bf16[2,96,768]{2,1,0:T(8,128)(2,1)S(1)}, u32[]{:S(2)}, u32[]{:S(2)}) collective-permute-start(bf16[2,96,768]{2,1,0:T(8,128)(2,1)S(1)} %pad_maximum_fusion.9), channel_id=1, source_target_pairs={{0,1},{1,0},{2,3},{3,2},{4,5},{5,4},{6,7},{7,6},{8,9},{9,8},{10,11... | collective-permute-start | bytes 884744 | tf_op jit(solution)/shard_map/ppermute | solution.py:89
  24.7 9.3 %collective-permute-start.4 = (bf16[2,96,768]{2,1,0:T(8,128)(2,1)S(1)}, bf16[2,96,768]{2,1,0:T(8,128)(2,1)S(1)}, u32[]{:S(2)}, u32[]{:S(2)}) collective-permute-start(bf16[2,96,768]{2,1,0:T(8,128)(2,1)S(1)} %pad_maximum_fusion.10), channel_id=1, source_target_pairs={{0,4},{4,0},{1,5},{5,1},{2,6},{6,2},{3,7},{7,3},{8,12},{12,8},{9,1... | collective-permute-start | bytes 884744 | tf_op jit(solution)/shard_map/ppermute | solution.py:89
  28.5 7.5 %collective-permute-start.7 = (bf16[2,96,768]{2,1,0:T(8,128)(2,1)S(1)}, bf16[2,96,768]{2,1,0:T(8,128)(2,1)S(1)}, u32[]{:S(2)}, u32[]{:S(2)}) collective-permute-start(bf16[2,96,768]{2,1,0:T(8,128)(2,1)S(1)} %pad_maximum_fusion.11), channel_id=1, source_target_pairs={{0,8},{8,0},{1,9},{9,1},{2,10},{10,2},{3,11},{11,3},{4,12},{12,4},... | collective-permute-start | bytes 884744 | tf_op jit(solution)/shard_map/ppermute | solution.py:89
  29.0 15.8 %collective-permute-start.2 = (bf16[4,96,768]{2,1,0:T(8,128)(2,1)S(1)}, bf16[4,96,768]{2,1,0:T(8,128)(2,1)}, u32[]{:S(2)}, u32[]{:S(2)}) collective-permute-start(bf16[4,96,768]{2,1,0:T(8,128)(2,1)S(1)} %pad_maximum_fusion.3), channel_id=1, source_target_pairs={{0,4},{4,0},{1,5},{5,1},{2,6},{6,2},{3,7},{7,3},{8,12},{12,8},{9,1... | collective-permute-start | bytes 1769480 | tf_op jit(solution)/shard_map/ppermute | solution.py:89
  34.9 14.0 %collective-permute-start.5 = (bf16[4,96,768]{2,1,0:T(8,128)(2,1)}, bf16[4,96,768]{2,1,0:T(8,128)(2,1)}, u32[]{:S(2)}, u32[]{:S(2)}) collective-permute-start(bf16[4,96,768]{2,1,0:T(8,128)(2,1)} %pad_maximum_fusion.4), channel_id=1, source_target_pairs={{0,8},{8,0},{1,9},{9,1},{2,10},{10,2},{3,11},{11,3},{4,12},{12,4},... | collective-permute-start | bytes 1769480 | tf_op jit(solution)/shard_map/ppermute | solution.py:89
  36.9 17.2 %collective-permute-start.8 = (bf16[4,96,768]{2,1,0:T(8,128)(2,1)}, bf16[4,96,768]{2,1,0:T(8,128)(2,1)}, u32[]{:S(2)}, u32[]{:S(2)}) collective-permute-start(bf16[4,96,768]{2,1,0:T(8,128)(2,1)} %pad_maximum_fusion.5), channel_id=1, source_target_pairs={{0,1},{1,0},{2,3},{3,2},{4,5},{5,4},{6,7},{7,6},{8,9},{9,8},{10,11... | collective-permute-start | bytes 1769480 | tf_op jit(solution)/shard_map/ppermute | solution.py:89
  38.4 18.1 %all-to-all-start = ((bf16[32,2,768]{2,1,0:T(2,128)(2,1)}), bf16[32,2,768]{2,1,0:T(2,128)(2,1)}, u32[]{:S(2)}, u32[]{:S(2)}) async-start(bf16[32,2,768]{2,1,0:T(2,128)(2,1)} %pad_maximum_fusion.15), calls=%async_computation | async-start | bytes 196608 | tf_op jit(solution)/shard_map/all_to_all | solution.py:1163
  51.3 26.1 %collective-permute-start.12 = (bf16[8,96,768]{2,1,0:T(8,128)(2,1)}, bf16[8,96,768]{2,1,0:T(8,128)(2,1)}, u32[]{:S(2)}, u32[]{:S(2)}) collective-permute-start(bf16[8,96,768]{2,1,0:T(8,128)(2,1)} %pad_maximum_fusion.1.refs_9_), channel_id=1, source_target_pairs={{0,1},{1,0},{2,3},{3,2},{4,5},{5,4},{6,7},{7,6},{8,9},{9,8},{10,11... | collective-permute-start | bytes 3538952 | tf_op jit(solution)/shard_map/ppermute | solution.py:89
  52.8 25.8 %collective-permute-start.9 = (bf16[8,96,768]{2,1,0:T(8,128)(2,1)}, bf16[8,96,768]{2,1,0:T(8,128)(2,1)}, u32[]{:S(2)}, u32[]{:S(2)}) collective-permute-start(bf16[8,96,768]{2,1,0:T(8,128)(2,1)} %pad_maximum_fusion.refs_5_), channel_id=1, source_target_pairs={{0,8},{8,0},{1,9},{9,1},{2,10},{10,2},{3,11},{11,3},{4,12},{12,4},... | collective-permute-start | bytes 3538952 | tf_op jit(solution)/shard_map/ppermute | solution.py:89
  60.3 25.8 %collective-permute-start.15 = (bf16[8,96,768]{2,1,0:T(8,128)(2,1)}, bf16[8,96,768]{2,1,0:T(8,128)(2,1)}, u32[]{:S(2)}, u32[]{:S(2)}) collective-permute-start(bf16[8,96,768]{2,1,0:T(8,128)(2,1)} %pad_maximum_fusion.2.refs_13_), channel_id=1, source_target_pairs={{0,4},{4,0},{1,5},{5,1},{2,6},{6,2},{3,7},{7,3},{8,12},{12,8},{9,1... | collective-permute-start | bytes 3538952 | tf_op jit(solution)/shard_map/ppermute | solution.py:89
  67.8 18.4 %collective-permute-start.10 = (bf16[8,96,768]{2,1,0:T(8,128)(2,1)}, bf16[8,96,768]{2,1,0:T(8,128)(2,1)S(1)}, u32[]{:S(2)}, u32[]{:S(2)}) collective-permute-start(bf16[8,96,768]{2,1,0:T(8,128)(2,1)} %pad_maximum_fusion.refs_5_), channel_id=1, source_target_pairs={{0,2},{2,0},{1,3},{3,1},{4,6},{6,4},{5,7},{7,5},{8,10},{10,8},{9,1... | collective-permute-start | bytes 3538952 | tf_op jit(solution)/shard_map/ppermute | solution.py:89
  67.8 19.6 %collective-permute-start.13 = (bf16[8,96,768]{2,1,0:T(8,128)(2,1)}, bf16[8,96,768]{2,1,0:T(8,128)(2,1)}, u32[]{:S(2)}, u32[]{:S(2)}) collective-permute-start(bf16[8,96,768]{2,1,0:T(8,128)(2,1)} %pad_maximum_fusion.1.refs_9_), channel_id=1, source_target_pairs={{0,2},{2,0},{1,3},{3,1},{4,6},{6,4},{5,7},{7,5},{8,10},{10,8},{9,1... | collective-permute-start | bytes 3538952 | tf_op jit(solution)/shard_map/ppermute | solution.py:89
  77.3 10.1 %collective-permute-start.16 = (bf16[8,96,768]{2,1,0:T(8,128)(2,1)}, bf16[8,96,768]{2,1,0:T(8,128)(2,1)}, u32[]{:S(2)}, u32[]{:S(2)}) collective-permute-start(bf16[8,96,768]{2,1,0:T(8,128)(2,1)} %pad_maximum_fusion.2.refs_13_), channel_id=1, source_target_pairs={{0,2},{2,0},{1,3},{3,1},{4,6},{6,4},{5,7},{7,5},{8,10},{10,8},{9,1... | collective-permute-start | bytes 3538952 | tf_op jit(solution)/shard_map/ppermute | solution.py:89
  78.6 8.8 %collective-permute-start.14 = (bf16[8,96,768]{2,1,0:T(8,128)(2,1)}, bf16[8,96,768]{2,1,0:T(8,128)(2,1)}, u32[]{:S(2)}, u32[]{:S(2)}) collective-permute-start(bf16[8,96,768]{2,1,0:T(8,128)(2,1)} %collective-permute-done.12.refs_10_), channel_id=1, source_target_pairs={{0,2},{2,0},{1,3},{3,1},{4,6},{6,4},{5,7},{7,5},{8,10},{10,8},{9,1... | collective-permute-start | bytes 3538952 | tf_op jit(solution)/shard_map/ppermute | solution.py:89
  86.1 4.9 %collective-permute-start.17 = (bf16[8,96,768]{2,1,0:T(8,128)(2,1)}, bf16[8,96,768]{2,1,0:T(8,128)(2,1)}, u32[]{:S(2)}, u32[]{:S(2)}) collective-permute-start(bf16[8,96,768]{2,1,0:T(8,128)(2,1)} %collective-permute-done.15.refs_14_), channel_id=1, source_target_pairs={{0,2},{2,0},{1,3},{3,1},{4,6},{6,4},{5,7},{7,5},{8,10},{10,8},{9,1... | collective-permute-start | bytes 3538952 | tf_op jit(solution)/shard_map/ppermute | solution.py:89
  104.8 6.0 %collective-permute-start.18 = (bf16[1,80,256]{2,1,0:T(8,128)(2,1)}, bf16[1,80,256]{2,1,0:T(8,128)(2,1)S(1)}, u32[]{:S(2)}, u32[]{:S(2)}) collective-permute-start(bf16[1,80,256]{2,1,0:T(8,128)(2,1)} %get-tuple-element.96), channel_id=1, source_target_pairs={{0,16},{16,0},{1,17},{17,1},{2,18},{18,2},{3,19},{19,3},{4,20},{20... | collective-permute-start | bytes 122888 | tf_op jit(solution)/shard_map/ppermute | solution.py:89
  107.9 7.9 %collective-permute-start.24 = (bf16[1,80,256]{2,1,0:T(8,128)(2,1)}, bf16[1,80,256]{2,1,0:T(8,128)(2,1)S(1)}, u32[]{:S(2)}, u32[]{:S(2)}) collective-permute-start(bf16[1,80,256]{2,1,0:T(8,128)(2,1)} %get-tuple-element.97), channel_id=1, source_target_pairs={{0,16},{16,0},{1,17},{17,1},{2,18},{18,2},{3,19},{19,3},{4,20},{20... | collective-permute-start | bytes 122888 | tf_op jit(solution)/shard_map/ppermute | solution.py:89
  108.0 7.0 %collective-permute-start.30 = (bf16[1,80,256]{2,1,0:T(8,128)(2,1)}, bf16[1,80,256]{2,1,0:T(8,128)(2,1)S(1)}, u32[]{:S(2)}, u32[]{:S(2)}) collective-permute-start(bf16[1,80,256]{2,1,0:T(8,128)(2,1)} %get-tuple-element.98), channel_id=1, source_target_pairs={{0,16},{16,0},{1,17},{17,1},{2,18},{18,2},{3,19},{19,3},{4,20},{20... | collective-permute-start | bytes 122888 | tf_op jit(solution)/shard_map/ppermute | solution.py:89
  115.8 4.5 %collective-permute-start.31 = (bf16[2,80,256]{2,1,0:T(8,128)(2,1)S(1)}, bf16[2,80,256]{2,1,0:T(8,128)(2,1)S(1)}, u32[]{:S(2)}, u32[]{:S(2)}) collective-permute-start(bf16[2,80,256]{2,1,0:T(8,128)(2,1)S(1)} %pad_maximum_fusion.18), channel_id=1, source_target_pairs={{0,8},{8,0},{1,9},{9,1},{2,10},{10,2},{3,11},{11,3},{4,12},{12,4},... | collective-permute-start | bytes 245768 | tf_op jit(solution)/shard_map/ppermute | solution.py:89
  116.6 5.5 %collective-permute-start.25 = (bf16[2,80,256]{2,1,0:T(8,128)(2,1)S(1)}, bf16[2,80,256]{2,1,0:T(8,128)(2,1)S(1)}, u32[]{:S(2)}, u32[]{:S(2)}) collective-permute-start(bf16[2,80,256]{2,1,0:T(8,128)(2,1)S(1)} %pad_maximum_fusion.17), channel_id=1, source_target_pairs={{0,4},{4,0},{1,5},{5,1},{2,6},{6,2},{3,7},{7,3},{8,12},{12,8},{9,1... | collective-permute-start | bytes 245768 | tf_op jit(solution)/shard_map/ppermute | solution.py:89
  117.9 5.4 %collective-permute-start.19 = (bf16[2,80,256]{2,1,0:T(8,128)(2,1)S(1)}, bf16[2,80,256]{2,1,0:T(8,128)(2,1)S(1)}, u32[]{:S(2)}, u32[]{:S(2)}) collective-permute-start(bf16[2,80,256]{2,1,0:T(8,128)(2,1)S(1)} %pad_maximum_fusion.16), channel_id=1, source_target_pairs={{0,1},{1,0},{2,3},{3,2},{4,5},{5,4},{6,7},{7,6},{8,9},{9,8},{10,11... | collective-permute-start | bytes 245768 | tf_op jit(solution)/shard_map/ppermute | solution.py:89
  120.3 5.5 %collective-permute-start.32 = (bf16[4,80,256]{2,1,0:T(8,128)(2,1)S(1)}, bf16[4,80,256]{2,1,0:T(8,128)(2,1)S(1)}, u32[]{:S(2)}, u32[]{:S(2)}) collective-permute-start(bf16[4,80,256]{2,1,0:T(8,128)(2,1)S(1)} %pad_maximum_fusion.14), channel_id=1, source_target_pairs={{0,1},{1,0},{2,3},{3,2},{4,5},{5,4},{6,7},{7,6},{8,9},{9,8},{10,11... | collective-permute-start | bytes 491528 | tf_op jit(solution)/shard_map/ppermute | solution.py:89
  122.2 5.4 %collective-permute-start.26 = (bf16[4,80,256]{2,1,0:T(8,128)(2,1)S(1)}, bf16[4,80,256]{2,1,0:T(8,128)(2,1)S(1)}, u32[]{:S(2)}, u32[]{:S(2)}) collective-permute-start(bf16[4,80,256]{2,1,0:T(8,128)(2,1)S(1)} %pad_maximum_fusion.13), channel_id=1, source_target_pairs={{0,8},{8,0},{1,9},{9,1},{2,10},{10,2},{3,11},{11,3},{4,12},{12,4},... | collective-permute-start | bytes 491528 | tf_op jit(solution)/shard_map/ppermute | solution.py:89
  123.2 5.4 %collective-permute-start.20 = (bf16[4,80,256]{2,1,0:T(8,128)(2,1)S(1)}, bf16[4,80,256]{2,1,0:T(8,128)(2,1)S(1)}, u32[]{:S(2)}, u32[]{:S(2)}) collective-permute-start(bf16[4,80,256]{2,1,0:T(8,128)(2,1)S(1)} %pad_maximum_fusion.12), channel_id=1, source_target_pairs={{0,4},{4,0},{1,5},{5,1},{2,6},{6,2},{3,7},{7,3},{8,12},{12,8},{9,1... | collective-permute-start | bytes 491528 | tf_op jit(solution)/shard_map/ppermute | solution.py:89
  125.9 5.0 %collective-permute-start.34 = (bf16[8,80,256]{2,1,0:T(8,128)(2,1)S(1)}, bf16[8,80,256]{2,1,0:T(8,128)(2,1)S(1)}, u32[]{:S(2)}, u32[]{:S(2)}) collective-permute-start(bf16[8,80,256]{2,1,0:T(8,128)(2,1)S(1)} %pad_maximum_fusion.8.refs_11_), channel_id=1, source_target_pairs={{0,2},{2,0},{1,3},{3,1},{4,6},{6,4},{5,7},{7,5},{8,10},{10,8},{9,1... | collective-permute-start | bytes 983048 | tf_op jit(solution)/shard_map/ppermute | solution.py:89
  125.9 10.2 %collective-permute-start.33 = (bf16[8,80,256]{2,1,0:T(8,128)(2,1)S(1)}, bf16[8,80,256]{2,1,0:T(8,128)(2,1)}, u32[]{:S(2)}, u32[]{:S(2)}) collective-permute-start(bf16[8,80,256]{2,1,0:T(8,128)(2,1)S(1)} %pad_maximum_fusion.8.refs_11_), channel_id=1, source_target_pairs={{0,4},{4,0},{1,5},{5,1},{2,6},{6,2},{3,7},{7,3},{8,12},{12,8},{9,1... | collective-permute-start | bytes 983048 | tf_op jit(solution)/shard_map/ppermute | solution.py:89
  127.6 9.4 %collective-permute-start.27 = (bf16[8,80,256]{2,1,0:T(8,128)(2,1)S(1)}, bf16[8,80,256]{2,1,0:T(8,128)(2,1)}, u32[]{:S(2)}, u32[]{:S(2)}) collective-permute-start(bf16[8,80,256]{2,1,0:T(8,128)(2,1)S(1)} %pad_maximum_fusion.7.refs_7_), channel_id=1, source_target_pairs={{0,1},{1,0},{2,3},{3,2},{4,5},{5,4},{6,7},{7,6},{8,9},{9,8},{10,11... | collective-permute-start | bytes 983048 | tf_op jit(solution)/shard_map/ppermute | solution.py:89
  128.7 9.7 %collective-permute-start.21 = (bf16[8,80,256]{2,1,0:T(8,128)(2,1)S(1)}, bf16[8,80,256]{2,1,0:T(8,128)(2,1)}, u32[]{:S(2)}, u32[]{:S(2)}) collective-permute-start(bf16[8,80,256]{2,1,0:T(8,128)(2,1)S(1)} %pad_maximum_fusion.6.refs_3_), channel_id=1, source_target_pairs={{0,8},{8,0},{1,9},{9,1},{2,10},{10,2},{3,11},{11,3},{4,12},{12,4},... | collective-permute-start | bytes 983048 | tf_op jit(solution)/shard_map/ppermute | solution.py:89
  130.8 8.3 %collective-permute-start.28 = (bf16[8,80,256]{2,1,0:T(8,128)(2,1)S(1)}, bf16[8,80,256]{2,1,0:T(8,128)(2,1)}, u32[]{:S(2)}, u32[]{:S(2)}) collective-permute-start(bf16[8,80,256]{2,1,0:T(8,128)(2,1)S(1)} %pad_maximum_fusion.7.refs_7_), channel_id=1, source_target_pairs={{0,2},{2,0},{1,3},{3,1},{4,6},{6,4},{5,7},{7,5},{8,10},{10,8},{9,1... | collective-permute-start | bytes 983048 | tf_op jit(solution)/shard_map/ppermute | solution.py:89
  130.9 8.3 %collective-permute-start.22 = (bf16[8,80,256]{2,1,0:T(8,128)(2,1)S(1)}, bf16[8,80,256]{2,1,0:T(8,128)(2,1)}, u32[]{:S(2)}, u32[]{:S(2)}) collective-permute-start(bf16[8,80,256]{2,1,0:T(8,128)(2,1)S(1)} %pad_maximum_fusion.6.refs_3_), channel_id=1, source_target_pairs={{0,2},{2,0},{1,3},{3,1},{4,6},{6,4},{5,7},{7,5},{8,10},{10,8},{9,1... | collective-permute-start | bytes 983048 | tf_op jit(solution)/shard_map/ppermute | solution.py:89
  149.5 14.0 %all-to-all-start.1 = ((f32[32,8,256]{2,1,0:T(8,128)}), f32[32,8,256]{2,1,0:T(8,128)S(1)}, u32[]{:S(2)}, u32[]{:S(2)}) async-start(f32[32,8,256]{2,1,0:T(8,128)} %get-tuple-element.99), calls=%async_computation.1 | async-start | bytes 524288 | tf_op jit(solution)/shard_map/all_to_all | solution.py:1271
  172.7 10.2 %collective-permute-start.42 = (bf16[8,64,256]{2,1,0:T(8,128)(2,1)S(1)}, bf16[8,64,256]{2,1,0:T(8,128)(2,1)S(1)}, u32[]{:S(2)}, u32[]{:S(2)}) collective-permute-start(bf16[8,64,256]{2,1,0:T(8,128)(2,1)S(1)} %get-tuple-element.108), channel_id=1, source_target_pairs={{0,2},{2,0},{1,3},{3,1},{4,6},{6,4},{5,7},{7,5},{8,10},{10,8},{9,1... | collective-permute-start | bytes 786440 | tf_op jit(solution)/shard_map/ppermute | solution.py:89
  173.1 11.3 %collective-permute-start.48 = (bf16[8,64,256]{2,1,0:T(8,128)(2,1)S(1)}, bf16[8,64,256]{2,1,0:T(8,128)(2,1)S(1)}, u32[]{:S(2)}, u32[]{:S(2)}) collective-permute-start(bf16[8,64,256]{2,1,0:T(8,128)(2,1)S(1)} %get-tuple-element.111), channel_id=1, source_target_pairs={{0,2},{2,0},{1,3},{3,1},{4,6},{6,4},{5,7},{7,5},{8,10},{10,8},{9,1... | collective-permute-start | bytes 786440 | tf_op jit(solution)/shard_map/ppermute | solution.py:89
  173.7 8.4 %collective-permute-start.38 = (bf16[8,64,256]{2,1,0:T(8,128)(2,1)S(1)}, bf16[8,64,256]{2,1,0:T(8,128)(2,1)S(1)}, u32[]{:S(2)}, u32[]{:S(2)}) collective-permute-start(bf16[8,64,256]{2,1,0:T(8,128)(2,1)S(1)} %add_convert_fusion.8), channel_id=1, source_target_pairs={{0,8},{8,0},{1,9},{9,1},{2,10},{10,2},{3,11},{11,3},{4,12},{12,4},... | collective-permute-start | bytes 786440 | tf_op jit(solution)/shard_map/ppermute | solution.py:89
  175.2 8.3 %collective-permute-start.44 = (bf16[8,64,256]{2,1,0:T(8,128)(2,1)S(1)}, bf16[8,64,256]{2,1,0:T(8,128)(2,1)S(1)}, u32[]{:S(2)}, u32[]{:S(2)}) collective-permute-start(bf16[8,64,256]{2,1,0:T(8,128)(2,1)S(1)} %add_convert_fusion.7), channel_id=1, source_target_pairs={{0,1},{1,0},{2,3},{3,2},{4,5},{5,4},{6,7},{7,6},{8,9},{9,8},{10,11... | collective-permute-start | bytes 786440 | tf_op jit(solution)/shard_map/ppermute | solution.py:89
  176.1 8.3 %collective-permute-start.50 = (bf16[8,64,256]{2,1,0:T(8,128)(2,1)S(1)}, bf16[8,64,256]{2,1,0:T(8,128)(2,1)S(1)}, u32[]{:S(2)}, u32[]{:S(2)}) collective-permute-start(bf16[8,64,256]{2,1,0:T(8,128)(2,1)S(1)} %add_convert_fusion.6), channel_id=1, source_target_pairs={{0,4},{4,0},{1,5},{5,1},{2,6},{6,2},{3,7},{7,3},{8,12},{12,8},{9,1... | collective-permute-start | bytes 786440 | tf_op jit(solution)/shard_map/ppermute | solution.py:89
  182.1 5.0 %collective-permute-start.39 = (bf16[4,64,256]{2,1,0:T(8,128)(2,1)S(1)}, bf16[4,64,256]{2,1,0:T(8,128)(2,1)S(1)}, u32[]{:S(2)}, u32[]{:S(2)}) collective-permute-start(bf16[4,64,256]{2,1,0:T(8,128)(2,1)S(1)} %add_convert_fusion.11), channel_id=1, source_target_pairs={{0,4},{4,0},{1,5},{5,1},{2,6},{6,2},{3,7},{7,3},{8,12},{12,8},{9,1... | collective-permute-start | bytes 393224 | tf_op jit(solution)/shard_map/ppermute | solution.py:89
  183.6 5.0 %collective-permute-start.45 = (bf16[4,64,256]{2,1,0:T(8,128)(2,1)S(1)}, bf16[4,64,256]{2,1,0:T(8,128)(2,1)S(1)}, u32[]{:S(2)}, u32[]{:S(2)}) collective-permute-start(bf16[4,64,256]{2,1,0:T(8,128)(2,1)S(1)} %add_convert_fusion.10), channel_id=1, source_target_pairs={{0,8},{8,0},{1,9},{9,1},{2,10},{10,2},{3,11},{11,3},{4,12},{12,4},... | collective-permute-start | bytes 393224 | tf_op jit(solution)/shard_map/ppermute | solution.py:89
  184.4 5.7 %collective-permute-start.51 = (bf16[4,64,256]{2,1,0:T(8,128)(2,1)S(1)}, bf16[4,64,256]{2,1,0:T(8,128)(2,1)S(1)}, u32[]{:S(2)}, u32[]{:S(2)}) collective-permute-start(bf16[4,64,256]{2,1,0:T(8,128)(2,1)S(1)} %add_convert_fusion.9), channel_id=1, source_target_pairs={{0,1},{1,0},{2,3},{3,2},{4,5},{5,4},{6,7},{7,6},{8,9},{9,8},{10,11... | collective-permute-start | bytes 393224 | tf_op jit(solution)/shard_map/ppermute | solution.py:89
  190.2 4.7 %collective-permute-start.52 = (bf16[2,64,256]{2,1,0:T(8,128)(2,1)S(1)}, bf16[2,64,256]{2,1,0:T(8,128)(2,1)S(1)}, u32[]{:S(2)}, u32[]{:S(2)}) collective-permute-start(bf16[2,64,256]{2,1,0:T(8,128)(2,1)S(1)} %add_convert_fusion.12), channel_id=1, source_target_pairs={{0,8},{8,0},{1,9},{9,1},{2,10},{10,2},{3,11},{11,3},{4,12},{12,4},... | collective-permute-start | bytes 196616 | tf_op jit(solution)/shard_map/ppermute | solution.py:89
  191.6 5.6 %collective-permute-start.41 = (bf16[1,64,256]{2,1,0:T(8,128)(2,1)S(1)}, bf16[1,64,256]{2,1,0:T(8,128)(2,1)S(1)}, u32[]{:S(2)}, u32[]{:S(2)}) collective-permute-start(bf16[1,64,256]{2,1,0:T(8,128)(2,1)S(1)} %add_convert_fusion.17), channel_id=1, source_target_pairs={{0,16},{16,0},{1,17},{17,1},{2,18},{18,2},{3,19},{19,3},{4,20},{20... | collective-permute-start | bytes 98312 | tf_op jit(solution)/shard_map/ppermute | solution.py:89
  193.0 5.2 %collective-permute-start.47 = (bf16[1,64,256]{2,1,0:T(8,128)(2,1)S(1)}, bf16[1,64,256]{2,1,0:T(8,128)(2,1)S(1)}, u32[]{:S(2)}, u32[]{:S(2)}) collective-permute-start(bf16[1,64,256]{2,1,0:T(8,128)(2,1)S(1)} %add_convert_fusion.16), channel_id=1, source_target_pairs={{0,16},{16,0},{1,17},{17,1},{2,18},{18,2},{3,19},{19,3},{4,20},{20... | collective-permute-start | bytes 98312 | tf_op jit(solution)/shard_map/ppermute | solution.py:89
  194.9 4.9 %collective-permute-start.53 = (bf16[1,64,256]{2,1,0:T(8,128)(2,1)S(1)}, bf16[1,64,256]{2,1,0:T(8,128)(2,1)S(1)}, u32[]{:S(2)}, u32[]{:S(2)}) collective-permute-start(bf16[1,64,256]{2,1,0:T(8,128)(2,1)S(1)} %add_convert_fusion.15), channel_id=1, source_target_pairs={{0,16},{16,0},{1,17},{17,1},{2,18},{18,2},{3,19},{19,3},{4,20},{20... | collective-permute-start | bytes 98312 | tf_op jit(solution)/shard_map/ppermute | solution.py:89
  221.9 6.4 %collective-permute-start.61 = (bf16[8,96,768]{2,1,0:T(8,128)(2,1)}, bf16[8,96,768]{2,1,0:T(8,128)(2,1)S(1)}, u32[]{:S(2)}, u32[]{:S(2)}) collective-permute-start(bf16[8,96,768]{2,1,0:T(8,128)(2,1)} %get-tuple-element.132), channel_id=1, source_target_pairs={{0,2},{2,0},{1,3},{3,1},{4,6},{6,4},{5,7},{7,5},{8,10},{10,8},{9,1... | collective-permute-start | bytes 3538952 | tf_op jit(solution)/shard_map/ppermute | solution.py:89
  222.4 9.3 %collective-permute-start.67 = (bf16[8,96,768]{2,1,0:T(8,128)(2,1)}, bf16[8,96,768]{2,1,0:T(8,128)(2,1)S(1)}, u32[]{:S(2)}, u32[]{:S(2)}) collective-permute-start(bf16[8,96,768]{2,1,0:T(8,128)(2,1)} %get-tuple-element.139), channel_id=1, source_target_pairs={{0,2},{2,0},{1,3},{3,1},{4,6},{6,4},{5,7},{7,5},{8,10},{10,8},{9,1... | collective-permute-start | bytes 3538952 | tf_op jit(solution)/shard_map/ppermute | solution.py:89
  222.5 11.5 %collective-permute-start.54 = (bf16[8,96,768]{2,1,0:T(8,128)(2,1)}, bf16[8,96,768]{2,1,0:T(8,128)(2,1)S(1)}, u32[]{:S(2)}, u32[]{:S(2)}) collective-permute-start(bf16[8,96,768]{2,1,0:T(8,128)(2,1)} %get-tuple-element.124), channel_id=1, source_target_pairs={{0,2},{2,0},{1,3},{3,1},{4,6},{6,4},{5,7},{7,5},{8,10},{10,8},{9,1... | collective-permute-start | bytes 3538952 | tf_op jit(solution)/shard_map/ppermute | solution.py:89
  222.9 36.6 %collective-permute-start.60 = (bf16[8,96,768]{2,1,0:T(8,128)(2,1)}, bf16[8,96,768]{2,1,0:T(8,128)(2,1)}, u32[]{:S(2)}, u32[]{:S(2)}) collective-permute-start(bf16[8,96,768]{2,1,0:T(8,128)(2,1)} %get-tuple-element.131), channel_id=1, source_target_pairs={{0,2},{2,0},{1,3},{3,1},{4,6},{6,4},{5,7},{7,5},{8,10},{10,8},{9,1... | collective-permute-start | bytes 3538952 | tf_op jit(solution)/shard_map/ppermute | solution.py:89
  224.9 38.7 %collective-permute-start.66 = (bf16[8,96,768]{2,1,0:T(8,128)(2,1)}, bf16[8,96,768]{2,1,0:T(8,128)(2,1)}, u32[]{:S(2)}, u32[]{:S(2)}) collective-permute-start(bf16[8,96,768]{2,1,0:T(8,128)(2,1)} %get-tuple-element.138), channel_id=1, source_target_pairs={{0,2},{2,0},{1,3},{3,1},{4,6},{6,4},{5,7},{7,5},{8,10},{10,8},{9,1... | collective-permute-start | bytes 3538952 | tf_op jit(solution)/shard_map/ppermute | solution.py:89
  228.3 28.3 %collective-permute-start.56 = (bf16[8,96,768]{2,1,0:T(8,128)(2,1)}, bf16[8,96,768]{2,1,0:T(8,128)(2,1)}, u32[]{:S(2)}, u32[]{:S(2)}) collective-permute-start(bf16[8,96,768]{2,1,0:T(8,128)(2,1)} %add_convert_fusion.2), channel_id=1, source_target_pairs={{0,8},{8,0},{1,9},{9,1},{2,10},{10,2},{3,11},{11,3},{4,12},{12,4},... | collective-permute-start | bytes 3538952 | tf_op jit(solution)/shard_map/ppermute | solution.py:89
  231.7 28.9 %collective-permute-start.62 = (bf16[8,96,768]{2,1,0:T(8,128)(2,1)}, bf16[8,96,768]{2,1,0:T(8,128)(2,1)}, u32[]{:S(2)}, u32[]{:S(2)}) collective-permute-start(bf16[8,96,768]{2,1,0:T(8,128)(2,1)} %add_convert_fusion.1), channel_id=1, source_target_pairs={{0,1},{1,0},{2,3},{3,2},{4,5},{5,4},{6,7},{7,6},{8,9},{9,8},{10,11... | collective-permute-start | bytes 3538952 | tf_op jit(solution)/shard_map/ppermute | solution.py:89
  234.0 29.7 %collective-permute-start.68 = (bf16[8,96,768]{2,1,0:T(8,128)(2,1)S(1)}, bf16[8,96,768]{2,1,0:T(8,128)(2,1)}, u32[]{:S(2)}, u32[]{:S(2)}) collective-permute-start(bf16[8,96,768]{2,1,0:T(8,128)(2,1)S(1)} %add_convert_fusion), channel_id=1, source_target_pairs={{0,4},{4,0},{1,5},{5,1},{2,6},{6,2},{3,7},{7,3},{8,12},{12,8},{9,1... | collective-permute-start | bytes 3538952 | tf_op jit(solution)/shard_map/ppermute | solution.py:89
  251.4 40.1 %all-to-all-start.2 = ((f32[32,1,288]{2,1,0:T(1,128)}), f32[32,1,288]{2,1,0:T(1,128)}, u32[]{:S(2)}, u32[]{:S(2)}) async-start(f32[32,1,288]{2,1,0:T(1,128)} %reshape.465), calls=%async_computation.2 | async-start | bytes 98304 | tf_op jit(solution)/shard_map/all_to_all | solution.py:1217
  258.3 16.7 %collective-permute-start.57 = (bf16[4,96,768]{2,1,0:T(8,128)(2,1)S(1)}, bf16[4,96,768]{2,1,0:T(8,128)(2,1)S(1)}, u32[]{:S(2)}, u32[]{:S(2)}) collective-permute-start(bf16[4,96,768]{2,1,0:T(8,128)(2,1)S(1)} %add_convert_fusion.5), channel_id=1, source_target_pairs={{0,4},{4,0},{1,5},{5,1},{2,6},{6,2},{3,7},{7,3},{8,12},{12,8},{9,1... | collective-permute-start | bytes 1769480 | tf_op jit(solution)/shard_map/ppermute | solution.py:89
  262.1 14.7 %collective-permute-start.63 = (bf16[4,96,768]{2,1,0:T(8,128)(2,1)S(1)}, bf16[4,96,768]{2,1,0:T(8,128)(2,1)S(1)}, u32[]{:S(2)}, u32[]{:S(2)}) collective-permute-start(bf16[4,96,768]{2,1,0:T(8,128)(2,1)S(1)} %add_convert_fusion.4), channel_id=1, source_target_pairs={{0,8},{8,0},{1,9},{9,1},{2,10},{10,2},{3,11},{11,3},{4,12},{12,4},... | collective-permute-start | bytes 1769480 | tf_op jit(solution)/shard_map/ppermute | solution.py:89
  265.1 16.3 %collective-permute-start.69 = (bf16[4,96,768]{2,1,0:T(8,128)(2,1)S(1)}, bf16[4,96,768]{2,1,0:T(8,128)(2,1)S(1)}, u32[]{:S(2)}, u32[]{:S(2)}) collective-permute-start(bf16[4,96,768]{2,1,0:T(8,128)(2,1)S(1)} %add_convert_fusion.3), channel_id=1, source_target_pairs={{0,1},{1,0},{2,3},{3,2},{4,5},{5,4},{6,7},{7,6},{8,9},{9,8},{10,11... | collective-permute-start | bytes 1769480 | tf_op jit(solution)/shard_map/ppermute | solution.py:89
  275.0 10.6 %collective-permute-start.58 = (bf16[2,96,768]{2,1,0:T(8,128)(2,1)S(1)}, bf16[2,96,768]{2,1,0:T(8,128)(2,1)S(1)}, u32[]{:S(2)}, u32[]{:S(2)}) collective-permute-start(bf16[2,96,768]{2,1,0:T(8,128)(2,1)S(1)} %fusion.10), channel_id=1, source_target_pairs={{0,1},{1,0},{2,3},{3,2},{4,5},{5,4},{6,7},{7,6},{8,9},{9,8},{10,11... | collective-permute-start | bytes 884744 | tf_op jit(solution)/shard_map/ppermute | solution.py:89
  276.8 10.7 %collective-permute-start.64 = (bf16[2,96,768]{2,1,0:T(8,128)(2,1)S(1)}, bf16[2,96,768]{2,1,0:T(8,128)(2,1)S(1)}, u32[]{:S(2)}, u32[]{:S(2)}) collective-permute-start(bf16[2,96,768]{2,1,0:T(8,128)(2,1)S(1)} %fusion.9), channel_id=1, source_target_pairs={{0,4},{4,0},{1,5},{5,1},{2,6},{6,2},{3,7},{7,3},{8,12},{12,8},{9,1... | collective-permute-start | bytes 884744 | tf_op jit(solution)/shard_map/ppermute | solution.py:89
  281.5 8.6 %collective-permute-start.70 = (bf16[2,96,768]{2,1,0:T(8,128)(2,1)S(1)}, bf16[2,96,768]{2,1,0:T(8,128)(2,1)S(1)}, u32[]{:S(2)}, u32[]{:S(2)}) collective-permute-start(bf16[2,96,768]{2,1,0:T(8,128)(2,1)S(1)} %fusion.8), channel_id=1, source_target_pairs={{0,8},{8,0},{1,9},{9,1},{2,10},{10,2},{3,11},{11,3},{4,12},{12,4},... | collective-permute-start | bytes 884744 | tf_op jit(solution)/shard_map/ppermute | solution.py:89
  286.4 21.0 %collective-permute-start.59 = (bf16[1,96,768]{2,1,0:T(8,128)(2,1)}, bf16[1,96,768]{2,1,0:T(8,128)(2,1)}, u32[]{:S(2)}, u32[]{:S(2)}) collective-permute-start(bf16[1,96,768]{2,1,0:T(8,128)(2,1)} %fusion.16), channel_id=1, source_target_pairs={{0,16},{16,0},{1,17},{17,1},{2,18},{18,2},{3,19},{19,3},{4,20},{20... | collective-permute-start | bytes 442376 | tf_op jit(solution)/shard_map/ppermute | solution.py:89
  288.3 19.1 %collective-permute-start.65 = (bf16[1,96,768]{2,1,0:T(8,128)(2,1)}, bf16[1,96,768]{2,1,0:T(8,128)(2,1)}, u32[]{:S(2)}, u32[]{:S(2)}) collective-permute-start(bf16[1,96,768]{2,1,0:T(8,128)(2,1)} %fusion.14), channel_id=1, source_target_pairs={{0,16},{16,0},{1,17},{17,1},{2,18},{18,2},{3,19},{19,3},{4,20},{20... | collective-permute-start | bytes 442376 | tf_op jit(solution)/shard_map/ppermute | solution.py:89
  291.5 15.8 %collective-permute-start.71 = (bf16[1,96,768]{2,1,0:T(8,128)(2,1)}, bf16[1,96,768]{2,1,0:T(8,128)(2,1)}, u32[]{:S(2)}, u32[]{:S(2)}) collective-permute-start(bf16[1,96,768]{2,1,0:T(8,128)(2,1)} %fusion.12), channel_id=1, source_target_pairs={{0,16},{16,0},{1,17},{17,1},{2,18},{18,2},{3,19},{19,3},{4,20},{20... | collective-permute-start | bytes 442376 | tf_op jit(solution)/shard_map/ppermute | solution.py:89
  (49 other events, 414.0 us)
where the time goes:
time: 315 us; the launch traced here: 311 us
  waiting for transfers between devices  93.1 us (30%)
  starting transfers between devices  80.4 us (26%)
  Pallas kernels  72.4 us (23%)
  other arithmetic  47.5 us (15%)
  local copies, waits for them, and re-layouts  15.6 us (5%)
    ppermute x72, waiting for transfers between devices, flip(): return lax.ppermute(value, name, [(0, 1), (1, 0)])  83.8 us
    ppermute x72, starting transfers between devices, flip(): return lax.ppermute(value, name, [(0, 1), (1, 0)])  67.8 us
    pallas_call x1, Pallas kernels, call_backward(): pl.pallas_call(functools.partial(backward_kernel, unit, seq_here), out_sh...  21.2 us
    pallas_call x1, Pallas kernels, call_embed(): pl.pallas_call(functools.partial(embed_kernel, picks), grid=(8,), out_sha...  14.9 us
    concatenate x18, other arithmetic, gather_relative(): jnp.concatenate([grown, flip(grown, name)])  14 us
    pallas_call x1, Pallas kernels, call_forward(): pl.pallas_call(functools.partial(forward_kernel, plan, devices // 4, seq_...  13.8 us
    convert_element_type x24, other arithmetic, reduce_relative(): sends[k] = add_terms(upper).astype(urgent.dtype)  12 us
    add x2, other arithmetic, adam_step(): return first_hat / (jnp.sqrt(second_hat) + adam_eps) + decay * weight  9.61 us
  transfers between devices with their start and end apart: 75, of which 41 were waited for; matrix products, arithmetic and copies ran while one was open for 19% of the time, Pallas kernels for 5%

commit v1 on v0

--- a/solution.py
+++ b/solution.py
@@ -115,11 +115,10 @@
     return held
 
 
-def bit_orders(names, core):
+def bit_orders(names, core, picks):
     outer = [name for name in names if name != core]
     count = len(outer)
     if count == 4:
-        picks = ((0, 3, 2, 1), (0, 2, 1, 3), (0, 1, 3, 2))
         return [[outer[k] for k in pick] + [core] for pick in picks]
     step = max(1, count // 3)
     return [outer[step * k :] + outer[: step * k] + [core] for k in range(3)]
@@ -129,31 +128,43 @@
     return 1 << (len(names) - 1 - names.index(name))
 
 
-def gather_relative(shards, orders, names, early=(), exchange=None, work=None):
+def gather_relative(shards, orders, names, early=(), exchange=None, work=None, split=False):
     held = []
     for number, (shard, order) in enumerate(zip(shards, orders)):
         grown, masks = shard, [0]
         for k, name in enumerate(order[:-2]):
-            grown = lax.optimization_barrier(jnp.concatenate([grown, flip(grown, name)]))
+            other, bit = flip(grown, name), device_mask(name, names)
+            pieces = [grown, other]
+            masks_all = [masks, [mask | bit for mask in masks]]
+            if split and k == len(order) - 3:
+                pieces = list(lax.optimization_barrier(pieces))
+                break
+            grown = lax.optimization_barrier(jnp.concatenate(pieces))
+            masks = sum(masks_all, [])
+            pieces, masks_all = [grown], [masks]
             if exchange is not None and k == 0 and number == len(orders) - 1:
                 grown, given = lax.optimization_barrier((grown, early[-1]))
                 early = (*early[:-1], exchange(given))
-            masks = masks + [mask | device_mask(name, names) for mask in masks]
-        held.append((grown, masks))
-    grown_all = [grown for grown, _ in held]
-    others = [flip(grown, order[-2]) for grown, order in zip(grown_all, orders)]
+                pieces = [grown]
+        held.append((pieces, masks_all))
+    grown_all = [pieces for pieces, _ in held]
+    others_all = [
+        [flip(piece, order[-2]) for piece in pieces] for pieces, order in zip(grown_all, orders)
+    ]
     if work is not None:
         late, early = lax.optimization_barrier((grown_all, early))
         grown_all, early = lax.optimization_barrier((late, work(*early)))
     gathered = []
-    for grown, other, (_, masks), order in zip(grown_all, others, held, orders):
+    for pieces, others, (_, masks_all), order in zip(grown_all, others_all, held, orders):
         bit = device_mask(order[-2], names)
-        pieces = [(grown, masks), (other, [mask | bit for mask in masks])]
+        pairs = list(zip(pieces, masks_all)) + [
+            (other, [mask | bit for mask in masks]) for other, masks in zip(others, masks_all)
+        ]
         bit = device_mask(order[-1], names)
-        pieces = pieces + [
-            (flip(piece, order[-1]), [mask | bit for mask in own]) for piece, own in pieces
+        pairs = pairs + [
+            (flip(piece, order[-1]), [mask | bit for mask in masks]) for piece, masks in pairs
         ]
-        gathered.append(pieces)
+        gathered.append(pairs)
     return gathered, early
 
 
@@ -1124,7 +1135,8 @@
     rows_here = seq_here * length
     devices = 2 ** len(names)
     me = lax.axis_index(names)
-    orders = bit_orders(names, core)
+    orders = bit_orders(names, core, ((0, 3, 2, 1), (0, 2, 1, 3), (0, 1, 3, 2)))
+    head_orders = bit_orders(names, core, ((3, 0, 1, 2), (0, 2, 3, 1), (0, 1, 2, 3)))
     slots = mlm_positions.shape[1]
     picks_here = seq_here * slots
     low = jnp.bfloat16
@@ -1172,23 +1184,27 @@
         return jnp.pad(embedding.astype(low), (0, over)).reshape(shifted_rows, width)
 
 
-    def unpack(small_all):
+    def unpack(small_all, first, last):
         starts = [sum(sizes[:k]) for k in range(len(sizes))]
-        vecs_all, labels_high, labels_low, pairs_high, pairs_low, quarter_all = (
-            small_all[:, 0, start : start + size] for start, size in zip(starts, sizes)
-        )
-        vec_rows = vecs_all.reshape(-1).astype(jnp.float32).reshape(-1, width)
-
-        def whole(high, small):
-            return (high.astype(jnp.int32) * 256 + small.astype(jnp.int32)).reshape(-1)
-
-        quarter_all = quarter_all.astype(jnp.int32).reshape(-1)
-        used = (jnp.arange(slots)[None, :] < quarter_all[:, None]).reshape(-1)
-        row_of = whole(labels_high, labels_low) - first_row
+        return [
+            small_all[:, 0, starts[k] : starts[k] + sizes[k]].reshape(-1)
+            for k in range(first, last)
+        ]
+
+    def unpack_layer(small_all):
+        (vecs_all,) = unpack(small_all, 0, 1)
         from_left = lax.dynamic_index_in_dim(small_all[:, 1], left, 0, False)
         from_right = lax.dynamic_index_in_dim(small_all[:, 1], right, 0, False)
         right_rows = jnp.pad(from_right, (width - over, over)).reshape(2, width)
-        return vec_rows, row_of, used, whole(pairs_high, pairs_low), from_left, right_rows
+        return vecs_all.astype(jnp.float32).reshape(-1, width), from_left, right_rows
+
+    def unpack_heads(small_all):
+        labels_high, labels_low, pairs_high, pairs_low, quarter_all = (
+            value.astype(jnp.int32) for value in unpack(small_all, 1, 6)
+        )
+        used = (jnp.arange(slots)[None, :] < quarter_all[:, None]).reshape(-1)
+        row_of = labels_high * 256 + labels_low - first_row
+        return row_of, used, pairs_high * 256 + pairs_low
 
     seq_start = jnp.arange(seq_here, dtype=jnp.int32) * length
 
@@ -1245,31 +1261,33 @@
         table_rows = -(-(shifted_rows + 1) // 128) * 128
 
         def prepare(embedding, small_all):
-            vec_rows, row_of, used, pairs_all, from_left, right_rows = unpack(small_all)
+            vec_rows, from_left, right_rows = unpack_layer(small_all)
             ends = jnp.pad(
                 jnp.concatenate([from_left[None], right_rows]).astype(jnp.float32),
                 ((0, 5), (0, 0)),
             )
-            labels = jnp.pad(
-                jnp.stack([row_of.astype(jnp.float32), used.astype(jnp.float32)]),
-                ((0, 6), (0, 0)),
-            )
             shifted = table_shard(embedding)
             table, owned = call_table(lone_shift, shifted, ends, table_rows, embed_here)
-            return table, owned, labels, vec_rows, pairs_all
-
-        gathered, (table, owned, labels, vec_rows, pairs_all) = gather_relative(
-            mats_low[:, None], orders, names, (embedding, small), share, prepare
+            return table, owned, vec_rows, small_all
+
+        gathered, (table, owned, vec_rows, small_all) = gather_relative(
+            mats_low[:, None], orders, names, (embedding, small), share, prepare, True
         )
         *heads, saved = call_forward(
             lone, span_lengths, places[None], tok_rows, vec_rows, gathered, devices, seq_here
         )
-        heads_all, _ = gather_relative(heads, orders, names)
+        heads_all, _ = gather_relative(heads, head_orders, names)
         picked, expo, stats, tops = call_logits(
             lone, lone_shift, table, heads_all, picks_here, embed_here, devices
         )
+        stats, small_all = lax.optimization_barrier((stats, small_all))
+        row_of, used, pairs_all = unpack_heads(small_all)
+        labels = jnp.pad(
+            jnp.stack([row_of.astype(jnp.float32), used.astype(jnp.float32)]), ((0, 6), (0, 0))
+        )
         stats = lax.all_to_all(stats, names, 0, 0, tiled=True)
-        plan = tuple(tuple(device_mask(name, names) for name in order) for order in back_orders)
+        head_back = [order[::-1] for order in head_orders]
+        plan = tuple(tuple(device_mask(name, names) for name in order) for order in head_back)
         scale, *sinks = call_terms(
             lone, stats, tops, expo, owned, labels, plan, picks_here
         )
@@ -1277,7 +1295,7 @@
             picked[:, picks_here : picks_here + seq_here].reshape(-1, width), pairs_all
         )
         d_parts, _ = reduce_relative(
-            sinks[0::3], list(zip(sinks[1::3], sinks[2::3])), back_orders
+            sinks[0::3], list(zip(sinks[1::3], sinks[2::3])), head_back
         )
         d_parts = [add_terms([term[0] for term in terms]) for terms in d_parts]
         top = jnp.concatenate(
@@ -1309,7 +1327,9 @@
         )
         grad_mats, step_mats = call_step(layer_mats, mom1_mats, mom2_mats, terms)
     else:
-        vec_rows, row_of, used, pairs_all, from_left, right_rows = unpack(share(small))
+        small_all = share(small)
+        vec_rows, from_left, right_rows = unpack_layer(small_all)
+        row_of, used, pairs_all = unpack_heads(small_all)
         same_row = (jnp.arange(width) < width - shift)[None, :]
         tall = jnp.concatenate(
             [from_left[None], table_shard(embedding), jnp.zeros((1, width), low)]

time: 315 us -> 313 us (level)
  waiting for transfers between devices: 93.1 us -> 105 us
  other arithmetic: 47.5 us -> 39.8 us
  starting transfers between devices: 80.4 us -> 75 us
    ppermute x72 -> x81, waiting for transfers between devices: 83.8 us -> 94.5 us  [flip(): return lax.ppermute(value, name, [(0, 1), (1, 0)])]
    concatenate x18 -> x15, other arithmetic: 14 us -> 7.96 us  [gather_relative(): grown = lax.optimization_barrier(jnp.concatenate(pieces))]
    ppermute x72 -> x81, starting transfers between devices: 67.8 us -> 62.4 us  [flip(): return lax.ppermute(value, name, [(0, 1), (1, 0)])]
  transfers between devices with their start and end apart: 75 -> 84, of which waited for: 41 -> 51; matrix products, arithmetic and copies ran while one was open for 19% -> 16% of each run, Pallas kernels for 5% -> 5%
where the time goes in v1:
time: 313 us; the launch traced here: 309 us
  waiting for transfers between devices  105 us (34%)
  starting transfers between devices  75 us (24%)
  Pallas kernels  72.3 us (23%)
  other arithmetic  39.8 us (13%)
  local copies, waits for them, and re-layouts  14.5 us (5%)
    ppermute x81, waiting for transfers between devices, flip(): return lax.ppermute(value, name, [(0, 1), (1, 0)])  94.5 us
    ppermute x81, starting transfers between devices, flip(): return lax.ppermute(value, name, [(0, 1), (1, 0)])  62.4 us
    pallas_call x1, Pallas kernels, call_backward(): pl.pallas_call(functools.partial(backward_kernel, unit, seq_here), out_sh...  21.2 us
    pallas_call x1, Pallas kernels, call_embed(): pl.pallas_call(functools.partial(embed_kernel, picks), grid=(8,), out_sha...  14.9 us
    pallas_call x1, Pallas kernels, call_forward(): pl.pallas_call(functools.partial(forward_kernel, plan, devices // 4, seq_...  13.8 us
    convert_element_type x24, other arithmetic, reduce_relative(): sends[k] = add_terms(upper).astype(urgent.dtype)  12 us
    add x2, other arithmetic, adam_step(): return first_hat / (jnp.sqrt(second_hat) + adam_eps) + decay * weight  9.61 us
    pallas_call x1, Pallas kernels, call_logits(): pl.pallas_call(functools.partial(logits_kernel, plan, embed_here, picks,...  9.05 us
  transfers between devices with their start and end apart: 84, of which 51 were waited for; matrix products, arithmetic and copies ran while one was open for 16% of the time, Pallas kernels for 5%

profile of v1, /device:TPU:0, one launch (start us, length us, event | category | flops | bytes accessed | tf_op | source)
XLA Modules:
  0.0 309.0 jit_solution(14618848087974319117)
XLA Ops:
  0.6 1.4 convert_element_type.609
  2.2 4.1 %collective-permute-start = (bf16[1,96,768]{2,1,0:T(8,128)(2,1)S(1)}, bf16[1,96,768]{2,1,0:T(8,128)(2,1)}, u32[]{:S(2)}, u32[]{:S(2)}) collective-permute-start(bf16[1,96,768]{2,1,0:T(8,128)(2,1)S(1)} %unstack.19), channel_id=1, source_target_pairs={{0,16},{16,0},{1,17},{17,1},{2,18},{18,2},{3,19},{19,3},{4,20},{20... | collective-permute-start | bytes 442376 | tf_op jit(solution)/shard_map/ppermute | solution.py:89
  6.7 3.0 collective-permute-start.6
  10.8 13.0 %collective-permute-done.3 = bf16[1,96,768]{2,1,0:T(8,128)(2,1)} collective-permute-done((bf16[1,96,768]{2,1,0:T(8,128)(2,1)S(1)}, bf16[1,96,768]{2,1,0:T(8,128)(2,1)}, u32[]{:S(2)}, u32[]{:S(2)}) %collective-permute-start.3) | collective-permute-done | bytes 147488 | tf_op jit(solution)/shard_map/ppermute | solution.py:89
  24.7 1.9 collective-permute-start.4
  27.6 1.6 collective-permute-start.1
  33.0 1.3 collective-permute-done.1
  35.7 1.4 collective-permute-start.5
  37.1 1.8 collective-permute-done.7
  39.8 5.7 %all-to-all-start = ((bf16[32,2,768]{2,1,0:T(2,128)(2,1)}), bf16[32,2,768]{2,1,0:T(2,128)(2,1)S(1)}, u32[]{:S(2)}, u32[]{:S(2)}) async-start(bf16[32,2,768]{2,1,0:T(2,128)(2,1)} %pad_maximum_fusion.12), calls=%async_computation | async-start | bytes 196608 | tf_op jit(solution)/shard_map/all_to_all | solution.py:1175
  45.5 2.0 collective-permute-done.2.refs_6_
  47.5 3.7 %collective-permute-start.9 = (bf16[4,96,768]{2,1,0:T(8,128)(2,1)}, bf16[4,96,768]{2,1,0:T(8,128)(2,1)}, u32[]{:S(2)}, u32[]{:S(2)}) collective-permute-start(bf16[4,96,768]{2,1,0:T(8,128)(2,1)} %pad_maximum_fusion.refs_5_), channel_id=1, source_target_pairs={{0,8},{8,0},{1,9},{9,1},{2,10},{10,2},{3,11},{11,3},{4,12},{12,4},... | collective-permute-start | bytes 1769480 | tf_op jit(solution)/shard_map/ppermute | solution.py:89
  51.3 1.7 collective-permute-done.5.refs_14_
  52.9 2.0 collective-permute-start.16
  55.7 1.8 all-to-all-done
  59.3 1.7 shard_map.189
  63.0 3.3 %collective-permute-done.9.refs_7_ = bf16[4,96,768]{2,1,0:T(8,128)(2,1)} collective-permute-done((bf16[4,96,768]{2,1,0:T(8,128)(2,1)}, bf16[4,96,768]{2,1,0:T(8,128)(2,1)}, u32[]{:S(2)}, u32[]{:S(2)}) %collective-permute-start.9) | collective-permute-done | bytes 589856 | tf_op jit(solution)/shard_map/ppermute | solution.py:89
  66.6 10.8 %collective-permute-done.10.refs_8_ = bf16[4,96,768]{2,1,0:T(8,128)(2,1)} collective-permute-done((bf16[4,96,768]{2,1,0:T(8,128)(2,1)}, bf16[4,96,768]{2,1,0:T(8,128)(2,1)}, u32[]{:S(2)}, u32[]{:S(2)}) %collective-permute-start.10) | collective-permute-done | bytes 589856 | tf_op jit(solution)/shard_map/ppermute | solution.py:89
  83.1 1.5 collective-permute-done.24.refs_26_
  84.8 1.5 collective-permute-done.13.refs_11_
  89.3 13.8 %shard_map.190 = (bf16[1,80,256]{2,1,0:T(8,128)(2,1)}, bf16[1,80,256]{2,1,0:T(8,128)(2,1)}, bf16[1,80,256]{2,1,0:T(8,128)(2,1)}, bf16[9216,768]{1,0:T(8,128)(2,1...) custom-call(s32[1]{0:T(128)} %bitcast.4.refs_0_.me_ref, ...), custom_call_target="tpu_custom_call" | custom-call | flops 3623878656 | bytes 50331648 | tf_op jit(solution)/shard_map/pallas_call | solution.py:560
  103.8 3.4 %collective-permute-start.33 = (bf16[1,80,256]{2,1,0:T(8,128)(2,1)}, bf16[1,80,256]{2,1,0:T(8,128)(2,1)S(1)}, u32[]{:S(2)}, u32[]{:S(2)}) collective-permute-start(bf16[1,80,256]{2,1,0:T(8,128)(2,1)} %get-tuple-element.122), channel_id=1, source_target_pairs={{0,16},{16,0},{1,17},{17,1},{2,18},{18,2},{3,19},{19,3},{4,20},{20... | collective-permute-start | bytes 122888 | tf_op jit(solution)/shard_map/ppermute | solution.py:89
  108.2 4.2 %collective-permute-done.39 = bf16[1,80,256]{2,1,0:T(8,128)(2,1)S(1)} collective-permute-done((bf16[1,80,256]{2,1,0:T(8,128)(2,1)}, bf16[1,80,256]{2,1,0:T(8,128)(2,1)S(1)}, u32[]{:S(2)}, u32[]{:S(2)}) %collective-permute-start.39) | collective-permute-done | bytes 40992 | tf_op jit(solution)/shard_map/ppermute | solution.py:89
  113.2 1.6 collective-permute-start.40
  115.6 1.6 collective-permute-start.34
  117.2 1.8 collective-permute-start.28
  121.2 2.1 collective-permute-done.28
  126.3 3.2 %collective-permute-done.29 = bf16[4,80,256]{2,1,0:T(8,128)(2,1)S(1)} collective-permute-done((bf16[4,80,256]{2,1,0:T(8,128)(2,1)S(1)}, bf16[4,80,256]{2,1,0:T(8,128)(2,1)S(1)}, u32[]{:S(2)}, u32[]{:S(2)}) %collective-permute-start.29) | collective-permute-done | bytes 163872 | tf_op jit(solution)/shard_map/ppermute | solution.py:89
  130.2 4.5 %collective-permute-done.42.refs_12_ = bf16[8,80,256]{2,1,0:T(8,128)(2,1)} collective-permute-done((bf16[8,80,256]{2,1,0:T(8,128)(2,1)S(1)}, bf16[8,80,256]{2,1,0:T(8,128)(2,1)}, u32[]{:S(2)}, u32[]{:S(2)}) %collective-permute-start.42) | collective-permute-done | bytes 327712 | tf_op jit(solution)/shard_map/ppermute | solution.py:89
  138.5 9.1 %shard_map.191 = (bf16[32,80,768]{2,1,0:T(8,128)(2,1)}, f32[2048,1024]{1,0:T(8,128)}, f32[32,8,256]{2,1,0:T(8,128)}, f32[8,256]{1,0:T(8,128)}) custom-call(s32[1]{0:T(128)} %bitcast.4.refs_0_.me_ref, s32[1]{0:T(128)} %bitcast.2.shift_ref.refs_1_, bf16[1024,768]{1,0:T(8,128)(2,1)} %copy-done.16, bf16[8,80,256]{2,1,0:T(8,128)(2,1)} %copy-done.35, ...), custom_call_target="tpu_custom_call" | custom-call | flops 3221225472 | bytes 16777216 | tf_op jit(solution)/shard_map/pallas_call | solution.py:765
  147.8 2.8 all-to-all-start.1
  152.6 8.8 %all-to-all-done.1.refs_0_ = f32[32,8,256]{2,1,0:T(8,128)S(1)} async-done(((f32[32,8,256]{2,1,0:T(8,128)}), f32[32,8,256]{2,1,0:T(8,128)S(1)}, u32[]{:S(2)}, u32[]{:S(2)}) %all-to-all-start.1) | async-done | bytes 262176 | tf_op jit(solution)/shard_map/all_to_all | solution.py:1288
  161.3 8.0 %shard_map.192 = (f32[8,2048]{1,0:T(8,128)S(1)}, bf16[16,64,256]{2,1,0:T(8,128)(2,1)S(1)}, bf16[8,64,256]{2,1,0:T(8,128)(2,1)S(1)}, bf16[8,64,256]{2,1,0:T(8,128...) custom-call(s32[1]{0:T(128)} %bitcast.4.refs_0_.me_ref, ...), custom_call_target="tpu_custom_call" | custom-call | flops 3221225472 | bytes 12582912 | tf_op jit(solution)/shard_map/pallas_call | solution.py:860
  174.7 5.1 %collective-permute-done.47 = bf16[8,64,256]{2,1,0:T(8,128)(2,1)S(1)} collective-permute-done((bf16[8,64,256]{2,1,0:T(8,128)(2,1)S(1)}, bf16[8,64,256]{2,1,0:T(8,128)(2,1)S(1)}, u32[]{:S(2)}, u32[]{:S(2)}) %collective-permute-start.47) | collective-permute-done | bytes 262176 | tf_op jit(solution)/shard_map/ppermute | solution.py:89
  183.3 1.7 collective-permute-done.48
  188.5 2.4 collective-permute-done.49
  192.5 2.5 collective-permute-start.62
  195.0 1.8 collective-permute-done.56
  198.1 21.2 %shard_map.193 = (f32[256,768]{1,0:T(8,128)}, f32[12,768]{1,0:T(8,128)}, bf16[16,96,768]{2,1,0:T(8,128)(2,1)}, bf16[8,96,768]{2,1,0:T(8,128)(2,1)}, bf16[8,96,76...) custom-call(s32[2]{0:T(128)} %refs_0_.1, ...), custom_call_target="tpu_custom_call" | custom-call | flops 7247757312 | bytes 50331648 | tf_op jit(solution)/shard_map/pallas_call | solution.py:599
  220.5 2.0 collective-permute-done.64
  222.6 2.8 add_convert_fusion.2
  225.8 1.4 collective-permute-start.65
  227.2 1.4 add_convert_fusion.1
  229.2 1.3 collective-permute-start.71
  231.9 14.9 %shard_map.194 = f32[954,768]{1,0:T(8,128)} custom-call(s32[1]{0:T(128)} %bitcast.2.shift_ref.refs_1_, f32[2048,1024]{1,0:T(8,128)} %get-tuple-element.172.refs_2_.expo_ref, f32[8,2048]{1,0:T(8,128)} %copy-done.17, f32[8,2048]{1,0:T(8,128)} %copy-done.15, bf16[32,80,768]{2,1,0:T(8,128)(2,1)} %get-tuple-element.174.picked_ref), custom_call_target="tpu_custom_call" | custom-call | flops 25769803776 | bytes 67108864 | tf_op jit(solution)/shard_map/pallas_call | solution.py:928
  246.8 1.5 reshape.470
  248.4 4.1 %all-to-all-start.2 = ((f32[32,1,288]{2,1,0:T(1,128)}), f32[32,1,288]{2,1,0:T(1,128)}, u32[]{:S(2)}, u32[]{:S(2)}) async-start(f32[32,1,288]{2,1,0:T(1,128)} %reshape.470), calls=%async_computation.2 | async-start | bytes 98304 | tf_op jit(solution)/shard_map/all_to_all | solution.py:1233
  252.5 1.6 collective-permute-done.65
  254.2 1.6 add_convert_fusion.5
  257.8 1.5 add_convert_fusion.4
  259.3 1.6 collective-permute-start.72
  260.9 1.5 add_convert_fusion.3
  263.3 1.4 convert_add_fusion.2.refs_3_
  264.8 1.4 convert_add_fusion.1.refs_7_
  266.2 1.6 convert_add_fusion.refs_11_
  267.8 4.2 %collective-permute-done.66.refs_4_ = bf16[4,96,768]{2,1,0:T(8,128)(2,1)S(1)} collective-permute-done((bf16[4,96,768]{2,1,0:T(8,128)(2,1)S(1)}, bf16[4,96,768]{2,1,0:T(8,128)(2,1)S(1)}, u32[]{:S(2)}, u32[]{:S(2)}) %collective-permute-start.66) | collective-permute-done | bytes 589856 | tf_op jit(solution)/shard_map/ppermute | solution.py:89
  272.1 1.3 collective-permute-start.67
  274.5 4.1 %collective-permute-done.78.refs_12_ = bf16[4,96,768]{2,1,0:T(8,128)(2,1)S(1)} collective-permute-done((bf16[4,96,768]{2,1,0:T(8,128)(2,1)S(1)}, bf16[4,96,768]{2,1,0:T(8,128)(2,1)S(1)}, u32[]{:S(2)}, u32[]{:S(2)}) %collective-permute-start.78) | collective-permute-done | bytes 589856 | tf_op jit(solution)/shard_map/ppermute | solution.py:89
  278.8 4.0 %collective-permute-done.67.refs_5_ = bf16[2,96,768]{2,1,0:T(8,128)(2,1)S(1)} collective-permute-done((bf16[2,96,768]{2,1,0:T(8,128)(2,1)S(1)}, bf16[2,96,768]{2,1,0:T(8,128)(2,1)S(1)}, u32[]{:S(2)}, u32[]{:S(2)}) %collective-permute-start.67) | collective-permute-done | bytes 294944 | tf_op jit(solution)/shard_map/ppermute | solution.py:89
  283.6 1.7 collective-permute-start.68
  288.7 1.7 collective-permute-start.80
  290.5 4.1 %reshape.452 = f32[732672]{0:T(1024)} reshape(f32[954,768]{1,0:T(8,128)} %shard_map.194) | data formatting | bytes 5861376 | tf_op jit(solution)/shard_map/reshape | solution.py:1229
  295.5 9.0 %fusion.5 = (f32[732528]{0:T(1024)}, f32[732528]{0:T(1024)}) fusion(f32[732528]{0:T(1024)} %param.21, f32[732528]{0:T(1024)} %param.27, f32[732528]{0:T(1024)} %param.26, f32[732672]{0:T(1024)} %reshape.452), kind=kLoop, calls=%fused_computation.6 | loop fusion | flops 9522864 | bytes 17580672 | tf_op jit(solution)/shard_map/add | solution.py:85
  305.3 3.5 %shard_map.195 = (f32[1728,128]{1,0:T(8,128)}, f32[1728,128]{1,0:T(8,128)}) custom-call(f32[1728,128]{1,0:T(8,128)S(1)} %bitcast.25, f32[1728,128]{1,0:T(8,128)S(1)} %bitcast.26, f32[1728,128]{1,0:T(8,128)S(1)} %bitcast.27, f32[4,96,768]{2,1,0:T(8,128)S(1)} %convert_add_fusion.2.refs_3_, bf16[4,96,768]{2,1,0:T(8,128)(2,1)S(1)} %copy-done.2, ...), custom_call_target="tpu_custom_call" | custom-call | tf_op jit(solution)/shard_map/pallas_call | solution.py:976
  (307 shorter events, 67.1 us)
Async XLA Ops:
  2.2 24.4 %collective-permute-start = (bf16[1,96,768]{2,1,0:T(8,128)(2,1)S(1)}, bf16[1,96,768]{2,1,0:T(8,128)(2,1)}, u32[]{:S(2)}, u32[]{:S(2)}) collective-permute-start(bf16[1,96,768]{2,1,0:T(8,128)(2,1)S(1)} %unstack.19), channel_id=1, source_target_pairs={{0,16},{16,0},{1,17},{17,1},{2,18},{18,2},{3,19},{19,3},{4,20},{20... | collective-permute-start | bytes 442376 | tf_op jit(solution)/shard_map/ppermute | solution.py:89
  6.5 17.3 %collective-permute-start.3 = (bf16[1,96,768]{2,1,0:T(8,128)(2,1)S(1)}, bf16[1,96,768]{2,1,0:T(8,128)(2,1)}, u32[]{:S(2)}, u32[]{:S(2)}) collective-permute-start(bf16[1,96,768]{2,1,0:T(8,128)(2,1)S(1)} %unstack.21), channel_id=1, source_target_pairs={{0,16},{16,0},{1,17},{17,1},{2,18},{18,2},{3,19},{19,3},{4,20},{20... | collective-permute-start | bytes 442376 | tf_op jit(solution)/shard_map/ppermute | solution.py:89
  6.7 23.3 %collective-permute-start.6 = (bf16[1,96,768]{2,1,0:T(8,128)(2,1)S(1)}, bf16[1,96,768]{2,1,0:T(8,128)(2,1)}, u32[]{:S(2)}, u32[]{:S(2)}) collective-permute-start(bf16[1,96,768]{2,1,0:T(8,128)(2,1)S(1)} %unstack.23), channel_id=1, source_target_pairs={{0,16},{16,0},{1,17},{17,1},{2,18},{18,2},{3,19},{19,3},{4,20},{20... | collective-permute-start | bytes 442376 | tf_op jit(solution)/shard_map/ppermute | solution.py:89
  24.7 7.4 %collective-permute-start.4 = (bf16[2,96,768]{2,1,0:T(8,128)(2,1)S(1)}, bf16[2,96,768]{2,1,0:T(8,128)(2,1)S(1)}, u32[]{:S(2)}, u32[]{:S(2)}) collective-permute-start(bf16[2,96,768]{2,1,0:T(8,128)(2,1)S(1)} %pad_maximum_fusion.7), channel_id=1, source_target_pairs={{0,4},{4,0},{1,5},{5,1},{2,6},{6,2},{3,7},{7,3},{8,12},{12,8},{9,1... | collective-permute-start | bytes 884744 | tf_op jit(solution)/shard_map/ppermute | solution.py:89
  27.6 6.8 %collective-permute-start.1 = (bf16[2,96,768]{2,1,0:T(8,128)(2,1)S(1)}, bf16[2,96,768]{2,1,0:T(8,128)(2,1)S(1)}, u32[]{:S(2)}, u32[]{:S(2)}) collective-permute-start(bf16[2,96,768]{2,1,0:T(8,128)(2,1)S(1)} %pad_maximum_fusion.6), channel_id=1, source_target_pairs={{0,1},{1,0},{2,3},{3,2},{4,5},{5,4},{6,7},{7,6},{8,9},{9,8},{10,11... | collective-permute-start | bytes 884744 | tf_op jit(solution)/shard_map/ppermute | solution.py:89
  31.0 7.9 %collective-permute-start.7 = (bf16[2,96,768]{2,1,0:T(8,128)(2,1)S(1)}, bf16[2,96,768]{2,1,0:T(8,128)(2,1)S(1)}, u32[]{:S(2)}, u32[]{:S(2)}) collective-permute-start(bf16[2,96,768]{2,1,0:T(8,128)(2,1)S(1)} %pad_maximum_fusion.8), channel_id=1, source_target_pairs={{0,8},{8,0},{1,9},{9,1},{2,10},{10,2},{3,11},{11,3},{4,12},{12,4},... | collective-permute-start | bytes 884744 | tf_op jit(solution)/shard_map/ppermute | solution.py:89
  35.2 12.3 %collective-permute-start.2 = (bf16[4,96,768]{2,1,0:T(8,128)(2,1)}, bf16[4,96,768]{2,1,0:T(8,128)(2,1)}, u32[]{:S(2)}, u32[]{:S(2)}) collective-permute-start(bf16[4,96,768]{2,1,0:T(8,128)(2,1)} %pad_maximum_fusion.refs_5_), channel_id=1, source_target_pairs={{0,4},{4,0},{1,5},{5,1},{2,6},{6,2},{3,7},{7,3},{8,12},{12,8},{9,1... | collective-permute-start | bytes 1769480 | tf_op jit(solution)/shard_map/ppermute | solution.py:89
  35.7 17.2 %collective-permute-start.5 = (bf16[4,96,768]{2,1,0:T(8,128)(2,1)}, bf16[4,96,768]{2,1,0:T(8,128)(2,1)}, u32[]{:S(2)}, u32[]{:S(2)}) collective-permute-start(bf16[4,96,768]{2,1,0:T(8,128)(2,1)} %pad_maximum_fusion.1.refs_13_), channel_id=1, source_target_pairs={{0,8},{8,0},{1,9},{9,1},{2,10},{10,2},{3,11},{11,3},{4,12},{12,4},... | collective-permute-start | bytes 1769480 | tf_op jit(solution)/shard_map/ppermute | solution.py:89
  39.7 15.2 %collective-permute-start.8 = (bf16[4,96,768]{2,1,0:T(8,128)(2,1)}, bf16[4,96,768]{2,1,0:T(8,128)(2,1)}, u32[]{:S(2)}, u32[]{:S(2)}) collective-permute-start(bf16[4,96,768]{2,1,0:T(8,128)(2,1)} %pad_maximum_fusion.2.refs_21_), channel_id=1, source_target_pairs={{0,1},{1,0},{2,3},{3,2},{4,5},{5,4},{6,7},{7,6},{8,9},{9,8},{10,11... | collective-permute-start | bytes 1769480 | tf_op jit(solution)/shard_map/ppermute | solution.py:89
  39.8 17.8 %all-to-all-start = ((bf16[32,2,768]{2,1,0:T(2,128)(2,1)}), bf16[32,2,768]{2,1,0:T(2,128)(2,1)S(1)}, u32[]{:S(2)}, u32[]{:S(2)}) async-start(bf16[32,2,768]{2,1,0:T(2,128)(2,1)} %pad_maximum_fusion.12), calls=%async_computation | async-start | bytes 196608 | tf_op jit(solution)/shard_map/all_to_all | solution.py:1175
  47.5 18.9 %collective-permute-start.9 = (bf16[4,96,768]{2,1,0:T(8,128)(2,1)}, bf16[4,96,768]{2,1,0:T(8,128)(2,1)}, u32[]{:S(2)}, u32[]{:S(2)}) collective-permute-start(bf16[4,96,768]{2,1,0:T(8,128)(2,1)} %pad_maximum_fusion.refs_5_), channel_id=1, source_target_pairs={{0,8},{8,0},{1,9},{9,1},{2,10},{10,2},{3,11},{11,3},{4,12},{12,4},... | collective-permute-start | bytes 1769480 | tf_op jit(solution)/shard_map/ppermute | solution.py:89
  51.2 26.1 %collective-permute-start.10 = (bf16[4,96,768]{2,1,0:T(8,128)(2,1)}, bf16[4,96,768]{2,1,0:T(8,128)(2,1)}, u32[]{:S(2)}, u32[]{:S(2)}) collective-permute-start(bf16[4,96,768]{2,1,0:T(8,128)(2,1)} %collective-permute-done.2.refs_6_), channel_id=1, source_target_pairs={{0,8},{8,0},{1,9},{9,1},{2,10},{10,2},{3,11},{11,3},{4,12},{12,4},... | collective-permute-start | bytes 1769480 | tf_op jit(solution)/shard_map/ppermute | solution.py:89
  52.9 24.5 %collective-permute-start.15 = (bf16[4,96,768]{2,1,0:T(8,128)(2,1)}, bf16[4,96,768]{2,1,0:T(8,128)(2,1)}, u32[]{:S(2)}, u32[]{:S(2)}) collective-permute-start(bf16[4,96,768]{2,1,0:T(8,128)(2,1)} %pad_maximum_fusion.1.refs_13_), channel_id=1, source_target_pairs={{0,1},{1,0},{2,3},{3,2},{4,5},{5,4},{6,7},{7,6},{8,9},{9,8},{10,11... | collective-permute-start | bytes 1769480 | tf_op jit(solution)/shard_map/ppermute | solution.py:89
  52.9 25.1 %collective-permute-start.16 = (bf16[4,96,768]{2,1,0:T(8,128)(2,1)}, bf16[4,96,768]{2,1,0:T(8,128)(2,1)}, u32[]{:S(2)}, u32[]{:S(2)}) collective-permute-start(bf16[4,96,768]{2,1,0:T(8,128)(2,1)} %collective-permute-done.5.refs_14_), channel_id=1, source_target_pairs={{0,1},{1,0},{2,3},{3,2},{4,5},{5,4},{6,7},{7,6},{8,9},{9,8},{10,11... | collective-permute-start | bytes 1769480 | tf_op jit(solution)/shard_map/ppermute | solution.py:89
  55.0 23.1 %collective-permute-start.21 = (bf16[4,96,768]{2,1,0:T(8,128)(2,1)}, bf16[4,96,768]{2,1,0:T(8,128)(2,1)}, u32[]{:S(2)}, u32[]{:S(2)}) collective-permute-start(bf16[4,96,768]{2,1,0:T(8,128)(2,1)} %pad_maximum_fusion.2.refs_21_), channel_id=1, source_target_pairs={{0,4},{4,0},{1,5},{5,1},{2,6},{6,2},{3,7},{7,3},{8,12},{12,8},{9,1... | collective-permute-start | bytes 1769480 | tf_op jit(solution)/shard_map/ppermute | solution.py:89
  66.4 12.3 %collective-permute-start.22 = (bf16[4,96,768]{2,1,0:T(8,128)(2,1)}, bf16[4,96,768]{2,1,0:T(8,128)(2,1)S(1)}, u32[]{:S(2)}, u32[]{:S(2)}) collective-permute-start(bf16[4,96,768]{2,1,0:T(8,128)(2,1)} %collective-permute-done.8.refs_22_), channel_id=1, source_target_pairs={{0,4},{4,0},{1,5},{5,1},{2,6},{6,2},{3,7},{7,3},{8,12},{12,8},{9,1... | collective-permute-start | bytes 1769480 | tf_op jit(solution)/shard_map/ppermute | solution.py:89
  79.6 5.1 %collective-permute-start.24 = (bf16[4,96,768]{2,1,0:T(8,128)(2,1)}, bf16[4,96,768]{2,1,0:T(8,128)(2,1)S(1)}, u32[]{:S(2)}, u32[]{:S(2)}) collective-permute-start(bf16[4,96,768]{2,1,0:T(8,128)(2,1)} %collective-permute-done.8.refs_22_), channel_id=1, source_target_pairs={{0,2},{2,0},{1,3},{3,1},{4,6},{6,4},{5,7},{7,5},{8,10},{10,8},{9,1... | collective-permute-start | bytes 1769480 | tf_op jit(solution)/shard_map/ppermute | solution.py:89
  80.4 5.9 %collective-permute-start.13 = (bf16[4,96,768]{2,1,0:T(8,128)(2,1)}, bf16[4,96,768]{2,1,0:T(8,128)(2,1)S(1)}, u32[]{:S(2)}, u32[]{:S(2)}) collective-permute-start(bf16[4,96,768]{2,1,0:T(8,128)(2,1)} %collective-permute-done.9.refs_7_), channel_id=1, source_target_pairs={{0,2},{2,0},{1,3},{3,1},{4,6},{6,4},{5,7},{7,5},{8,10},{10,8},{9,1... | collective-permute-start | bytes 1769480 | tf_op jit(solution)/shard_map/ppermute | solution.py:89
  81.3 6.9 %collective-permute-start.14 = (bf16[4,96,768]{2,1,0:T(8,128)(2,1)}, bf16[4,96,768]{2,1,0:T(8,128)(2,1)}, u32[]{:S(2)}, u32[]{:S(2)}) collective-permute-start(bf16[4,96,768]{2,1,0:T(8,128)(2,1)} %collective-permute-done.10.refs_8_), channel_id=1, source_target_pairs={{0,2},{2,0},{1,3},{3,1},{4,6},{6,4},{5,7},{7,5},{8,10},{10,8},{9,1... | collective-permute-start | bytes 1769480 | tf_op jit(solution)/shard_map/ppermute | solution.py:89
  82.1 6.0 %collective-permute-start.19 = (bf16[4,96,768]{2,1,0:T(8,128)(2,1)}, bf16[4,96,768]{2,1,0:T(8,128)(2,1)}, u32[]{:S(2)}, u32[]{:S(2)}) collective-permute-start(bf16[4,96,768]{2,1,0:T(8,128)(2,1)} %collective-permute-done.15.refs_15_), channel_id=1, source_target_pairs={{0,2},{2,0},{1,3},{3,1},{4,6},{6,4},{5,7},{7,5},{8,10},{10,8},{9,1... | collective-permute-start | bytes 1769480 | tf_op jit(solution)/shard_map/ppermute | solution.py:89
  83.0 5.2 %collective-permute-start.20 = (bf16[4,96,768]{2,1,0:T(8,128)(2,1)}, bf16[4,96,768]{2,1,0:T(8,128)(2,1)}, u32[]{:S(2)}, u32[]{:S(2)}) collective-permute-start(bf16[4,96,768]{2,1,0:T(8,128)(2,1)} %collective-permute-done.16.refs_16_), channel_id=1, source_target_pairs={{0,2},{2,0},{1,3},{3,1},{4,6},{6,4},{5,7},{7,5},{8,10},{10,8},{9,1... | collective-permute-start | bytes 1769480 | tf_op jit(solution)/shard_map/ppermute | solution.py:89
  103.8 11.0 %collective-permute-start.33 = (bf16[1,80,256]{2,1,0:T(8,128)(2,1)}, bf16[1,80,256]{2,1,0:T(8,128)(2,1)S(1)}, u32[]{:S(2)}, u32[]{:S(2)}) collective-permute-start(bf16[1,80,256]{2,1,0:T(8,128)(2,1)} %get-tuple-element.122), channel_id=1, source_target_pairs={{0,16},{16,0},{1,17},{17,1},{2,18},{18,2},{3,19},{19,3},{4,20},{20... | collective-permute-start | bytes 122888 | tf_op jit(solution)/shard_map/ppermute | solution.py:89
  107.2 5.2 %collective-permute-start.39 = (bf16[1,80,256]{2,1,0:T(8,128)(2,1)}, bf16[1,80,256]{2,1,0:T(8,128)(2,1)S(1)}, u32[]{:S(2)}, u32[]{:S(2)}) collective-permute-start(bf16[1,80,256]{2,1,0:T(8,128)(2,1)} %get-tuple-element.123), channel_id=1, source_target_pairs={{0,16},{16,0},{1,17},{17,1},{2,18},{18,2},{3,19},{19,3},{4,20},{20... | collective-permute-start | bytes 122888 | tf_op jit(solution)/shard_map/ppermute | solution.py:89
  113.2 5.7 %collective-permute-start.40 = (bf16[2,80,256]{2,1,0:T(8,128)(2,1)S(1)}, bf16[2,80,256]{2,1,0:T(8,128)(2,1)S(1)}, u32[]{:S(2)}, u32[]{:S(2)}) collective-permute-start(bf16[2,80,256]{2,1,0:T(8,128)(2,1)S(1)} %pad_maximum_fusion.15), channel_id=1, source_target_pairs={{0,8},{8,0},{1,9},{9,1},{2,10},{10,2},{3,11},{11,3},{4,12},{12,4},... | collective-permute-start | bytes 245768 | tf_op jit(solution)/shard_map/ppermute | solution.py:89
  117.2 6.2 %collective-permute-start.28 = (bf16[2,80,256]{2,1,0:T(8,128)(2,1)S(1)}, bf16[2,80,256]{2,1,0:T(8,128)(2,1)S(1)}, u32[]{:S(2)}, u32[]{:S(2)}) collective-permute-start(bf16[2,80,256]{2,1,0:T(8,128)(2,1)S(1)} %pad_maximum_fusion.13), channel_id=1, source_target_pairs={{0,16},{16,0},{1,17},{17,1},{2,18},{18,2},{3,19},{19,3},{4,20},{20... | collective-permute-start | bytes 245768 | tf_op jit(solution)/shard_map/ppermute | solution.py:89
  119.0 5.4 %collective-permute-start.41 = (bf16[4,80,256]{2,1,0:T(8,128)(2,1)S(1)}, bf16[4,80,256]{2,1,0:T(8,128)(2,1)S(1)}, u32[]{:S(2)}, u32[]{:S(2)}) collective-permute-start(bf16[4,80,256]{2,1,0:T(8,128)(2,1)S(1)} %pad_maximum_fusion.11), channel_id=1, source_target_pairs={{0,4},{4,0},{1,5},{5,1},{2,6},{6,2},{3,7},{7,3},{8,12},{12,8},{9,1... | collective-permute-start | bytes 491528 | tf_op jit(solution)/shard_map/ppermute | solution.py:89
  120.1 5.4 %collective-permute-start.35 = (bf16[4,80,256]{2,1,0:T(8,128)(2,1)S(1)}, bf16[4,80,256]{2,1,0:T(8,128)(2,1)S(1)}, u32[]{:S(2)}, u32[]{:S(2)}) collective-permute-start(bf16[4,80,256]{2,1,0:T(8,128)(2,1)S(1)} %pad_maximum_fusion.10), channel_id=1, source_target_pairs={{0,1},{1,0},{2,3},{3,2},{4,5},{5,4},{6,7},{7,6},{8,9},{9,8},{10,11... | collective-permute-start | bytes 491528 | tf_op jit(solution)/shard_map/ppermute | solution.py:89
  123.3 6.2 %collective-permute-start.29 = (bf16[4,80,256]{2,1,0:T(8,128)(2,1)S(1)}, bf16[4,80,256]{2,1,0:T(8,128)(2,1)S(1)}, u32[]{:S(2)}, u32[]{:S(2)}) collective-permute-start(bf16[4,80,256]{2,1,0:T(8,128)(2,1)S(1)} %pad_maximum_fusion.9), channel_id=1, source_target_pairs={{0,8},{8,0},{1,9},{9,1},{2,10},{10,2},{3,11},{11,3},{4,12},{12,4},... | collective-permute-start | bytes 491528 | tf_op jit(solution)/shard_map/ppermute | solution.py:89
  124.4 5.4 %collective-permute-start.43 = (bf16[8,80,256]{2,1,0:T(8,128)(2,1)S(1)}, bf16[8,80,256]{2,1,0:T(8,128)(2,1)S(1)}, u32[]{:S(2)}, u32[]{:S(2)}) collective-permute-start(bf16[8,80,256]{2,1,0:T(8,128)(2,1)S(1)} %pad_maximum_fusion.5.refs_11_), channel_id=1, source_target_pairs={{0,2},{2,0},{1,3},{3,1},{4,6},{6,4},{5,7},{7,5},{8,10},{10,8},{9,1... | collective-permute-start | bytes 983048 | tf_op jit(solution)/shard_map/ppermute | solution.py:89
  124.5 10.2 %collective-permute-start.42 = (bf16[8,80,256]{2,1,0:T(8,128)(2,1)S(1)}, bf16[8,80,256]{2,1,0:T(8,128)(2,1)}, u32[]{:S(2)}, u32[]{:S(2)}) collective-permute-start(bf16[8,80,256]{2,1,0:T(8,128)(2,1)S(1)} %pad_maximum_fusion.5.refs_11_), channel_id=1, source_target_pairs={{0,1},{1,0},{2,3},{3,2},{4,5},{5,4},{6,7},{7,6},{8,9},{9,8},{10,11... | collective-permute-start | bytes 983048 | tf_op jit(solution)/shard_map/ppermute | solution.py:89
  125.5 10.3 %collective-permute-start.36 = (bf16[8,80,256]{2,1,0:T(8,128)(2,1)S(1)}, bf16[8,80,256]{2,1,0:T(8,128)(2,1)}, u32[]{:S(2)}, u32[]{:S(2)}) collective-permute-start(bf16[8,80,256]{2,1,0:T(8,128)(2,1)S(1)} %pad_maximum_fusion.4.refs_7_), channel_id=1, source_target_pairs={{0,8},{8,0},{1,9},{9,1},{2,10},{10,2},{3,11},{11,3},{4,12},{12,4},... | collective-permute-start | bytes 983048 | tf_op jit(solution)/shard_map/ppermute | solution.py:89
  129.6 7.1 %collective-permute-start.30 = (bf16[8,80,256]{2,1,0:T(8,128)(2,1)S(1)}, bf16[8,80,256]{2,1,0:T(8,128)(2,1)S(1)}, u32[]{:S(2)}, u32[]{:S(2)}) collective-permute-start(bf16[8,80,256]{2,1,0:T(8,128)(2,1)S(1)} %pad_maximum_fusion.3.refs_3_), channel_id=1, source_target_pairs={{0,4},{4,0},{1,5},{5,1},{2,6},{6,2},{3,7},{7,3},{8,12},{12,8},{9,1... | collective-permute-start | bytes 983048 | tf_op jit(solution)/shard_map/ppermute | solution.py:89
  129.7 7.8 %collective-permute-start.37 = (bf16[8,80,256]{2,1,0:T(8,128)(2,1)S(1)}, bf16[8,80,256]{2,1,0:T(8,128)(2,1)}, u32[]{:S(2)}, u32[]{:S(2)}) collective-permute-start(bf16[8,80,256]{2,1,0:T(8,128)(2,1)S(1)} %pad_maximum_fusion.4.refs_7_), channel_id=1, source_target_pairs={{0,2},{2,0},{1,3},{3,1},{4,6},{6,4},{5,7},{7,5},{8,10},{10,8},{9,1... | collective-permute-start | bytes 983048 | tf_op jit(solution)/shard_map/ppermute | solution.py:89
  129.8 7.7 %collective-permute-start.31 = (bf16[8,80,256]{2,1,0:T(8,128)(2,1)S(1)}, bf16[8,80,256]{2,1,0:T(8,128)(2,1)}, u32[]{:S(2)}, u32[]{:S(2)}) collective-permute-start(bf16[8,80,256]{2,1,0:T(8,128)(2,1)S(1)} %pad_maximum_fusion.3.refs_3_), channel_id=1, source_target_pairs={{0,2},{2,0},{1,3},{3,1},{4,6},{6,4},{5,7},{7,5},{8,10},{10,8},{9,1... | collective-permute-start | bytes 983048 | tf_op jit(solution)/shard_map/ppermute | solution.py:89
  147.8 13.5 %all-to-all-start.1 = ((f32[32,8,256]{2,1,0:T(8,128)}), f32[32,8,256]{2,1,0:T(8,128)S(1)}, u32[]{:S(2)}, u32[]{:S(2)}) async-start(f32[32,8,256]{2,1,0:T(8,128)} %get-tuple-element.126), calls=%async_computation.1 | async-start | bytes 524288 | tf_op jit(solution)/shard_map/all_to_all | solution.py:1288
  170.5 10.2 %collective-permute-start.51 = (bf16[8,64,256]{2,1,0:T(8,128)(2,1)S(1)}, bf16[8,64,256]{2,1,0:T(8,128)(2,1)S(1)}, u32[]{:S(2)}, u32[]{:S(2)}) collective-permute-start(bf16[8,64,256]{2,1,0:T(8,128)(2,1)S(1)} %get-tuple-element.135), channel_id=1, source_target_pairs={{0,2},{2,0},{1,3},{3,1},{4,6},{6,4},{5,7},{7,5},{8,10},{10,8},{9,1... | collective-permute-start | bytes 786440 | tf_op jit(solution)/shard_map/ppermute | solution.py:89
  170.9 11.4 %collective-permute-start.57 = (bf16[8,64,256]{2,1,0:T(8,128)(2,1)S(1)}, bf16[8,64,256]{2,1,0:T(8,128)(2,1)S(1)}, u32[]{:S(2)}, u32[]{:S(2)}) collective-permute-start(bf16[8,64,256]{2,1,0:T(8,128)(2,1)S(1)} %get-tuple-element.138), channel_id=1, source_target_pairs={{0,2},{2,0},{1,3},{3,1},{4,6},{6,4},{5,7},{7,5},{8,10},{10,8},{9,1... | collective-permute-start | bytes 786440 | tf_op jit(solution)/shard_map/ppermute | solution.py:89
  171.5 8.4 %collective-permute-start.47 = (bf16[8,64,256]{2,1,0:T(8,128)(2,1)S(1)}, bf16[8,64,256]{2,1,0:T(8,128)(2,1)S(1)}, u32[]{:S(2)}, u32[]{:S(2)}) collective-permute-start(bf16[8,64,256]{2,1,0:T(8,128)(2,1)S(1)} %add_convert_fusion.8), channel_id=1, source_target_pairs={{0,4},{4,0},{1,5},{5,1},{2,6},{6,2},{3,7},{7,3},{8,12},{12,8},{9,1... | collective-permute-start | bytes 786440 | tf_op jit(solution)/shard_map/ppermute | solution.py:89
  173.0 8.3 %collective-permute-start.53 = (bf16[8,64,256]{2,1,0:T(8,128)(2,1)S(1)}, bf16[8,64,256]{2,1,0:T(8,128)(2,1)S(1)}, u32[]{:S(2)}, u32[]{:S(2)}) collective-permute-start(bf16[8,64,256]{2,1,0:T(8,128)(2,1)S(1)} %add_convert_fusion.7), channel_id=1, source_target_pairs={{0,8},{8,0},{1,9},{9,1},{2,10},{10,2},{3,11},{11,3},{4,12},{12,4},... | collective-permute-start | bytes 786440 | tf_op jit(solution)/shard_map/ppermute | solution.py:89
  173.6 8.7 %collective-permute-start.59 = (bf16[8,64,256]{2,1,0:T(8,128)(2,1)S(1)}, bf16[8,64,256]{2,1,0:T(8,128)(2,1)S(1)}, u32[]{:S(2)}, u32[]{:S(2)}) collective-permute-start(bf16[8,64,256]{2,1,0:T(8,128)(2,1)S(1)} %add_convert_fusion.6), channel_id=1, source_target_pairs={{0,1},{1,0},{2,3},{3,2},{4,5},{5,4},{6,7},{7,6},{8,9},{9,8},{10,11... | collective-permute-start | bytes 786440 | tf_op jit(solution)/shard_map/ppermute | solution.py:89
  179.9 5.0 %collective-permute-start.48 = (bf16[4,64,256]{2,1,0:T(8,128)(2,1)S(1)}, bf16[4,64,256]{2,1,0:T(8,128)(2,1)S(1)}, u32[]{:S(2)}, u32[]{:S(2)}) collective-permute-start(bf16[4,64,256]{2,1,0:T(8,128)(2,1)S(1)} %add_convert_fusion.11), channel_id=1, source_target_pairs={{0,8},{8,0},{1,9},{9,1},{2,10},{10,2},{3,11},{11,3},{4,12},{12,4},... | collective-permute-start | bytes 393224 | tf_op jit(solution)/shard_map/ppermute | solution.py:89
  181.4 5.0 %collective-permute-start.54 = (bf16[4,64,256]{2,1,0:T(8,128)(2,1)S(1)}, bf16[4,64,256]{2,1,0:T(8,128)(2,1)S(1)}, u32[]{:S(2)}, u32[]{:S(2)}) collective-permute-start(bf16[4,64,256]{2,1,0:T(8,128)(2,1)S(1)} %add_convert_fusion.10), channel_id=1, source_target_pairs={{0,1},{1,0},{2,3},{3,2},{4,5},{5,4},{6,7},{7,6},{8,9},{9,8},{10,11... | collective-permute-start | bytes 393224 | tf_op jit(solution)/shard_map/ppermute | solution.py:89
  182.4 5.0 %collective-permute-start.60 = (bf16[4,64,256]{2,1,0:T(8,128)(2,1)S(1)}, bf16[4,64,256]{2,1,0:T(8,128)(2,1)S(1)}, u32[]{:S(2)}, u32[]{:S(2)}) collective-permute-start(bf16[4,64,256]{2,1,0:T(8,128)(2,1)S(1)} %add_convert_fusion.9), channel_id=1, source_target_pairs={{0,4},{4,0},{1,5},{5,1},{2,6},{6,2},{3,7},{7,3},{8,12},{12,8},{9,1... | collective-permute-start | bytes 393224 | tf_op jit(solution)/shard_map/ppermute | solution.py:89
  185.0 5.9 %collective-permute-start.49 = (bf16[2,64,256]{2,1,0:T(8,128)(2,1)S(1)}, bf16[2,64,256]{2,1,0:T(8,128)(2,1)S(1)}, u32[]{:S(2)}, u32[]{:S(2)}) collective-permute-start(bf16[2,64,256]{2,1,0:T(8,128)(2,1)S(1)} %add_convert_fusion.14), channel_id=1, source_target_pairs={{0,16},{16,0},{1,17},{17,1},{2,18},{18,2},{3,19},{19,3},{4,20},{20... | collective-permute-start | bytes 196616 | tf_op jit(solution)/shard_map/ppermute | solution.py:89
  186.5 5.3 %collective-permute-start.55 = (bf16[2,64,256]{2,1,0:T(8,128)(2,1)S(1)}, bf16[2,64,256]{2,1,0:T(8,128)(2,1)S(1)}, u32[]{:S(2)}, u32[]{:S(2)}) collective-permute-start(bf16[2,64,256]{2,1,0:T(8,128)(2,1)S(1)} %add_convert_fusion.13), channel_id=1, source_target_pairs={{0,4},{4,0},{1,5},{5,1},{2,6},{6,2},{3,7},{7,3},{8,12},{12,8},{9,1... | collective-permute-start | bytes 196616 | tf_op jit(solution)/shard_map/ppermute | solution.py:89
  187.4 5.0 %collective-permute-start.61 = (bf16[2,64,256]{2,1,0:T(8,128)(2,1)S(1)}, bf16[2,64,256]{2,1,0:T(8,128)(2,1)S(1)}, u32[]{:S(2)}, u32[]{:S(2)}) collective-permute-start(bf16[2,64,256]{2,1,0:T(8,128)(2,1)S(1)} %add_convert_fusion.12), channel_id=1, source_target_pairs={{0,8},{8,0},{1,9},{9,1},{2,10},{10,2},{3,11},{11,3},{4,12},{12,4},... | collective-permute-start | bytes 196616 | tf_op jit(solution)/shard_map/ppermute | solution.py:89
  219.4 6.4 %collective-permute-start.70 = (bf16[8,96,768]{2,1,0:T(8,128)(2,1)}, bf16[8,96,768]{2,1,0:T(8,128)(2,1)S(1)}, u32[]{:S(2)}, u32[]{:S(2)}) collective-permute-start(bf16[8,96,768]{2,1,0:T(8,128)(2,1)} %get-tuple-element.158), channel_id=1, source_target_pairs={{0,2},{2,0},{1,3},{3,1},{4,6},{6,4},{5,7},{7,5},{8,10},{10,8},{9,1... | collective-permute-start | bytes 3538952 | tf_op jit(solution)/shard_map/ppermute | solution.py:89
  219.9 9.3 %collective-permute-start.76 = (bf16[8,96,768]{2,1,0:T(8,128)(2,1)}, bf16[8,96,768]{2,1,0:T(8,128)(2,1)S(1)}, u32[]{:S(2)}, u32[]{:S(2)}) collective-permute-start(bf16[8,96,768]{2,1,0:T(8,128)(2,1)} %get-tuple-element.165), channel_id=1, source_target_pairs={{0,2},{2,0},{1,3},{3,1},{4,6},{6,4},{5,7},{7,5},{8,10},{10,8},{9,1... | collective-permute-start | bytes 3538952 | tf_op jit(solution)/shard_map/ppermute | solution.py:89
  220.0 10.9 %collective-permute-start.63 = (bf16[8,96,768]{2,1,0:T(8,128)(2,1)}, bf16[8,96,768]{2,1,0:T(8,128)(2,1)S(1)}, u32[]{:S(2)}, u32[]{:S(2)}) collective-permute-start(bf16[8,96,768]{2,1,0:T(8,128)(2,1)} %get-tuple-element.150), channel_id=1, source_target_pairs={{0,2},{2,0},{1,3},{3,1},{4,6},{6,4},{5,7},{7,5},{8,10},{10,8},{9,1... | collective-permute-start | bytes 3538952 | tf_op jit(solution)/shard_map/ppermute | solution.py:89
  220.4 36.4 %collective-permute-start.69 = (bf16[8,96,768]{2,1,0:T(8,128)(2,1)}, bf16[8,96,768]{2,1,0:T(8,128)(2,1)}, u32[]{:S(2)}, u32[]{:S(2)}) collective-permute-start(bf16[8,96,768]{2,1,0:T(8,128)(2,1)} %get-tuple-element.157), channel_id=1, source_target_pairs={{0,2},{2,0},{1,3},{3,1},{4,6},{6,4},{5,7},{7,5},{8,10},{10,8},{9,1... | collective-permute-start | bytes 3538952 | tf_op jit(solution)/shard_map/ppermute | solution.py:89
  222.5 38.4 %collective-permute-start.75 = (bf16[8,96,768]{2,1,0:T(8,128)(2,1)}, bf16[8,96,768]{2,1,0:T(8,128)(2,1)}, u32[]{:S(2)}, u32[]{:S(2)}) collective-permute-start(bf16[8,96,768]{2,1,0:T(8,128)(2,1)} %get-tuple-element.164), channel_id=1, source_target_pairs={{0,2},{2,0},{1,3},{3,1},{4,6},{6,4},{5,7},{7,5},{8,10},{10,8},{9,1... | collective-permute-start | bytes 3538952 | tf_op jit(solution)/shard_map/ppermute | solution.py:89
  225.8 28.3 %collective-permute-start.65 = (bf16[8,96,768]{2,1,0:T(8,128)(2,1)}, bf16[8,96,768]{2,1,0:T(8,128)(2,1)}, u32[]{:S(2)}, u32[]{:S(2)}) collective-permute-start(bf16[8,96,768]{2,1,0:T(8,128)(2,1)} %add_convert_fusion.2), channel_id=1, source_target_pairs={{0,8},{8,0},{1,9},{9,1},{2,10},{10,2},{3,11},{11,3},{4,12},{12,4},... | collective-permute-start | bytes 3538952 | tf_op jit(solution)/shard_map/ppermute | solution.py:89
  229.2 28.6 %collective-permute-start.71 = (bf16[8,96,768]{2,1,0:T(8,128)(2,1)}, bf16[8,96,768]{2,1,0:T(8,128)(2,1)}, u32[]{:S(2)}, u32[]{:S(2)}) collective-permute-start(bf16[8,96,768]{2,1,0:T(8,128)(2,1)} %add_convert_fusion.1), channel_id=1, source_target_pairs={{0,1},{1,0},{2,3},{3,2},{4,5},{5,4},{6,7},{7,6},{8,9},{9,8},{10,11... | collective-permute-start | bytes 3538952 | tf_op jit(solution)/shard_map/ppermute | solution.py:89
  230.9 30.0 %collective-permute-start.77 = (bf16[8,96,768]{2,1,0:T(8,128)(2,1)S(1)}, bf16[8,96,768]{2,1,0:T(8,128)(2,1)}, u32[]{:S(2)}, u32[]{:S(2)}) collective-permute-start(bf16[8,96,768]{2,1,0:T(8,128)(2,1)S(1)} %add_convert_fusion), channel_id=1, source_target_pairs={{0,4},{4,0},{1,5},{5,1},{2,6},{6,2},{3,7},{7,3},{8,12},{12,8},{9,1... | collective-permute-start | bytes 3538952 | tf_op jit(solution)/shard_map/ppermute | solution.py:89
  248.4 40.4 %all-to-all-start.2 = ((f32[32,1,288]{2,1,0:T(1,128)}), f32[32,1,288]{2,1,0:T(1,128)}, u32[]{:S(2)}, u32[]{:S(2)}) async-start(f32[32,1,288]{2,1,0:T(1,128)} %reshape.470), calls=%async_computation.2 | async-start | bytes 98304 | tf_op jit(solution)/shard_map/all_to_all | solution.py:1233
  255.8 16.3 %collective-permute-start.66 = (bf16[4,96,768]{2,1,0:T(8,128)(2,1)S(1)}, bf16[4,96,768]{2,1,0:T(8,128)(2,1)S(1)}, u32[]{:S(2)}, u32[]{:S(2)}) collective-permute-start(bf16[4,96,768]{2,1,0:T(8,128)(2,1)S(1)} %add_convert_fusion.5), channel_id=1, source_target_pairs={{0,4},{4,0},{1,5},{5,1},{2,6},{6,2},{3,7},{7,3},{8,12},{12,8},{9,1... | collective-permute-start | bytes 1769480 | tf_op jit(solution)/shard_map/ppermute | solution.py:89
  259.3 14.4 %collective-permute-start.72 = (bf16[4,96,768]{2,1,0:T(8,128)(2,1)S(1)}, bf16[4,96,768]{2,1,0:T(8,128)(2,1)S(1)}, u32[]{:S(2)}, u32[]{:S(2)}) collective-permute-start(bf16[4,96,768]{2,1,0:T(8,128)(2,1)S(1)} %add_convert_fusion.4), channel_id=1, source_target_pairs={{0,8},{8,0},{1,9},{9,1},{2,10},{10,2},{3,11},{11,3},{4,12},{12,4},... | collective-permute-start | bytes 1769480 | tf_op jit(solution)/shard_map/ppermute | solution.py:89
  262.3 16.3 %collective-permute-start.78 = (bf16[4,96,768]{2,1,0:T(8,128)(2,1)S(1)}, bf16[4,96,768]{2,1,0:T(8,128)(2,1)S(1)}, u32[]{:S(2)}, u32[]{:S(2)}) collective-permute-start(bf16[4,96,768]{2,1,0:T(8,128)(2,1)S(1)} %add_convert_fusion.3), channel_id=1, source_target_pairs={{0,1},{1,0},{2,3},{3,2},{4,5},{5,4},{6,7},{7,6},{8,9},{9,8},{10,11... | collective-permute-start | bytes 1769480 | tf_op jit(solution)/shard_map/ppermute | solution.py:89
  272.1 10.7 %collective-permute-start.67 = (bf16[2,96,768]{2,1,0:T(8,128)(2,1)S(1)}, bf16[2,96,768]{2,1,0:T(8,128)(2,1)S(1)}, u32[]{:S(2)}, u32[]{:S(2)}) collective-permute-start(bf16[2,96,768]{2,1,0:T(8,128)(2,1)S(1)} %fusion.10), channel_id=1, source_target_pairs={{0,1},{1,0},{2,3},{3,2},{4,5},{5,4},{6,7},{7,6},{8,9},{9,8},{10,11... | collective-permute-start | bytes 884744 | tf_op jit(solution)/shard_map/ppermute | solution.py:89
  273.7 11.6 %collective-permute-start.73 = (bf16[2,96,768]{2,1,0:T(8,128)(2,1)S(1)}, bf16[2,96,768]{2,1,0:T(8,128)(2,1)S(1)}, u32[]{:S(2)}, u32[]{:S(2)}) collective-permute-start(bf16[2,96,768]{2,1,0:T(8,128)(2,1)S(1)} %fusion.9), channel_id=1, source_target_pairs={{0,4},{4,0},{1,5},{5,1},{2,6},{6,2},{3,7},{7,3},{8,12},{12,8},{9,1... | collective-permute-start | bytes 884744 | tf_op jit(solution)/shard_map/ppermute | solution.py:89
  278.7 8.6 %collective-permute-start.79 = (bf16[2,96,768]{2,1,0:T(8,128)(2,1)S(1)}, bf16[2,96,768]{2,1,0:T(8,128)(2,1)S(1)}, u32[]{:S(2)}, u32[]{:S(2)}) collective-permute-start(bf16[2,96,768]{2,1,0:T(8,128)(2,1)S(1)} %fusion.8), channel_id=1, source_target_pairs={{0,8},{8,0},{1,9},{9,1},{2,10},{10,2},{3,11},{11,3},{4,12},{12,4},... | collective-permute-start | bytes 884744 | tf_op jit(solution)/shard_map/ppermute | solution.py:89
  283.6 21.6 %collective-permute-start.68 = (bf16[1,96,768]{2,1,0:T(8,128)(2,1)}, bf16[1,96,768]{2,1,0:T(8,128)(2,1)}, u32[]{:S(2)}, u32[]{:S(2)}) collective-permute-start(bf16[1,96,768]{2,1,0:T(8,128)(2,1)} %fusion.16), channel_id=1, source_target_pairs={{0,16},{16,0},{1,17},{17,1},{2,18},{18,2},{3,19},{19,3},{4,20},{20... | collective-permute-start | bytes 442376 | tf_op jit(solution)/shard_map/ppermute | solution.py:89
  286.1 19.1 %collective-permute-start.74 = (bf16[1,96,768]{2,1,0:T(8,128)(2,1)}, bf16[1,96,768]{2,1,0:T(8,128)(2,1)}, u32[]{:S(2)}, u32[]{:S(2)}) collective-permute-start(bf16[1,96,768]{2,1,0:T(8,128)(2,1)} %fusion.14), channel_id=1, source_target_pairs={{0,16},{16,0},{1,17},{17,1},{2,18},{18,2},{3,19},{19,3},{4,20},{20... | collective-permute-start | bytes 442376 | tf_op jit(solution)/shard_map/ppermute | solution.py:89
  288.7 16.4 %collective-permute-start.80 = (bf16[1,96,768]{2,1,0:T(8,128)(2,1)}, bf16[1,96,768]{2,1,0:T(8,128)(2,1)}, u32[]{:S(2)}, u32[]{:S(2)}) collective-permute-start(bf16[1,96,768]{2,1,0:T(8,128)(2,1)} %fusion.12), channel_id=1, source_target_pairs={{0,16},{16,0},{1,17},{17,1},{2,18},{18,2},{3,19},{19,3},{4,20},{20... | collective-permute-start | bytes 442376 | tf_op jit(solution)/shard_map/ppermute | solution.py:89
  (66 other events, 403.0 us)
